TPU v7x, 128 devices: a whole 4x4x4 slice. The times are simulated.
128 devices in a mesh: role: 16 (over z, y_hi, core), tp: 8 (over y_lo, x).
Axes of the slice: x: 4, y: 4 (y_hi: 2, y_lo: 2; y = y_hi * 2 + y_lo), z: 4, core: 2. Of those that a mesh axis runs over, the one named last changes fastest.
Arguments:
- x_pre: bfloat16 [22528, 8192], P('role'), may hold values from -6 to 6
- ln_gain: bfloat16 [8192], replicated, may hold values from 0.25 to 1.75
- w_kv: bfloat16 [8192, 2048], P('role', 'tp'), may hold values from -0.0625 to 0.0625
- kv_bias: bfloat16 [2048], P('tp'), may hold values from -3 to 3
- page_owner: int32 [176, 1], P('role'), may hold values from 0 to 15; in each aligned block of 11 rows (0 to 10, 11 to 21, ...) at most 2 rows name the same one
- page_req: int32 [176], P('role'), may hold values from 0 to 31
- kv_pool: bfloat16 [512, 128, 2048], P('role', None, 'tp'), may hold values from -6 to 6
- block_table: int32 [512, 4], P('role'), may hold values from 0 to 31
- cache_len: int32 [512], P('role'), may hold values from 1 to 512, 131072 in all
- dec_q: bfloat16 [4, 512, 8192], P(None, 'role', 'tp'), may hold values from -100 to 100
- dec_kv: bfloat16 [4, 512, 2048], P(None, 'role', 'tp'), may hold values from -6 to 6
- w_out: bfloat16 [8192, 8192], P('tp', 'role'), may hold values from -0.0625 to 0.0625
Outputs:
- decoded: bfloat16 [4, 512, 8192], P(None, 'tp', 'role')
Inputs may be any that keep to these rules, and one draw needn't show every extreme that they name: `page_owner`: of the 11 pages of one role index, at most 2 belong to requests of one owner, and this bound is reached.
All inputs are finite; a program needn't handle non-finite values. No bound on the sum of `cache_len` on one device may be relied on, other than what follows from the above.
Results may differ from a plain program's by a relative error of at most 0.0054.
Values may be sent and summed in bfloat16 or wider, within the bound.
A program may use at most 128 MiB of HBM per device.

v0:
```python
import math

import jax
import jax.numpy as jnp
from jax import lax
from jax.sharding import PartitionSpec as P

QH = 64
KVH = 8
HS = 128
PAGE = 128


EPSILON = 1e-06


def body(
    x_pre,
    ln_gain,
    w_kv,
    kv_bias,
    page_owner,
    page_req,
    kv_pool,
    block_table,
    cache_len,
    dec_q,
    dec_kv,
    w_out,
):
    activations = x_pre.astype(jnp.float32)
    inverse = lax.rsqrt(jnp.mean(activations * activations, axis=-1, keepdims=True) + EPSILON)
    normed = (activations * inverse * ln_gain.astype(jnp.float32)).astype(jnp.bfloat16)
    kv_width = w_kv.shape[1]
    projected = jnp.dot(
        normed, lax.all_gather(w_kv, "role", axis=0, tiled=True), preferred_element_type=jnp.float32
    )
    fresh_kv = (projected + kv_bias.astype(jnp.float32)).astype(jnp.bfloat16)
    page_count = page_req.shape[0]
    page_blocks = fresh_kv.reshape(page_count, PAGE, kv_width)
    owners = page_owner[:, 0]
    tags = jnp.stack([owners, page_req], axis=1).astype(jnp.bfloat16)
    got_pages, got_tags = (
        lax.all_gather(page_blocks, "role", axis=0, tiled=True),
        lax.all_gather(tags, "role", axis=0, tiled=True),
    )
    whole_tags = got_tags.astype(jnp.int32)
    slot_request = jnp.where(whole_tags[:, 0] == lax.axis_index("role"), whole_tags[:, 1], -1)
    steps_count = dec_q.shape[0]
    requests = dec_q.shape[1]
    kv_dev = kv_width // (2 * HS)
    per_kv = QH // KVH
    rows_q = steps_count * per_kv
    scaling = 1.0 / math.sqrt(HS)
    queries = (
        dec_q.reshape(steps_count, requests, kv_dev, per_kv, HS)
        .transpose(1, 2, 0, 3, 4)
        .reshape(requests, kv_dev, rows_q, HS)
    )
    cache_kv = kv_pool[block_table].reshape(requests, -1, kv_dev, 2, HS)
    positions = jnp.arange(cache_kv.shape[1])
    is_live = positions[None, :] < cache_len[:, None]
    cache_scores = (
        jnp.einsum(
            "rgqd,rtgd->rgqt", queries, cache_kv[:, :, :, 0], preferred_element_type=jnp.float32
        )
        * scaling
    )
    cache_scores = jnp.where(is_live[:, None, None, :], cache_scores, -jnp.inf)
    own_kv = dec_kv.reshape(steps_count, requests, kv_dev, 2, HS)
    own_scores = (
        jnp.einsum(
            "rgqd,srgd->rgqs", queries, own_kv[:, :, :, 0], preferred_element_type=jnp.float32
        )
        * scaling
    )
    row_step = jnp.arange(rows_q) // per_kv
    causal = jnp.arange(steps_count)[None, :] <= row_step[:, None]
    own_scores = jnp.where(causal[None, None], own_scores, -jnp.inf)
    slot_count = got_pages.shape[0]
    slot_kv = got_pages.reshape(slot_count, PAGE, kv_dev, 2, HS)
    is_valid = slot_request >= 0
    onehot = slot_request[:, None] == jnp.arange(requests)[None, :]
    slot_queries = jnp.einsum(
        "mr,rgqd->mgqd", onehot.astype(jnp.bfloat16), queries, preferred_element_type=jnp.float32
    ).astype(jnp.bfloat16)
    slot_scores = (
        jnp.einsum(
            "mgqd,mtgd->mgqt", slot_queries, slot_kv[:, :, :, 0], preferred_element_type=jnp.float32
        )
        * scaling
    )
    slot_top = jnp.max(slot_scores, axis=-1)
    page_top = jnp.max(jnp.where(onehot[:, :, None, None], slot_top[:, None], -jnp.inf), axis=0)
    row_top = jnp.maximum(
        jnp.maximum(jnp.max(cache_scores, axis=-1), jnp.max(own_scores, axis=-1)), page_top
    )
    slot_row_top = jnp.sum(jnp.where(onehot[:, :, None, None], row_top[None], 0.0), axis=1)
    cache_weights = jnp.where(
        is_live[:, None, None, :], jnp.exp(cache_scores - row_top[..., None]), 0.0
    )
    own_weights = jnp.where(causal[None, None], jnp.exp(own_scores - row_top[..., None]), 0.0)
    slot_weights = jnp.where(
        is_valid[:, None, None, None], jnp.exp(slot_scores - slot_row_top[..., None]), 0.0
    )
    onehot_float = onehot.astype(jnp.float32)
    weight_sum = jnp.sum(cache_weights, axis=-1) + jnp.sum(own_weights, axis=-1)
    weight_sum = weight_sum + jnp.einsum(
        "mr,mgq->rgq", onehot_float, jnp.sum(slot_weights, axis=-1), precision=lax.Precision.HIGHEST
    )
    accumulated = jnp.einsum(
        "rgqt,rtgd->rgqd",
        cache_weights.astype(jnp.bfloat16),
        cache_kv[:, :, :, 1],
        preferred_element_type=jnp.float32,
    )
    accumulated = accumulated + jnp.einsum(
        "rgqs,srgd->rgqd",
        own_weights.astype(jnp.bfloat16),
        own_kv[:, :, :, 1],
        preferred_element_type=jnp.float32,
    )
    slot_terms = jnp.einsum(
        "mgqt,mtgd->mgqd",
        slot_weights.astype(jnp.bfloat16),
        slot_kv[:, :, :, 1],
        preferred_element_type=jnp.float32,
    )
    accumulated = accumulated + jnp.einsum(
        "mr,mgqd->rgqd", onehot_float, slot_terms, precision=lax.Precision.HIGHEST
    )
    attention = accumulated / weight_sum[..., None]
    attended = attention.reshape(requests, kv_dev, steps_count, per_kv, HS).transpose(2, 0, 1, 3, 4)
    attended = attended.reshape(steps_count, requests, kv_dev * per_kv * HS).astype(jnp.bfloat16)
    partial_terms = jnp.einsum(
        "srk,kc->src",
        lax.all_gather(attended, "role", axis=1, tiled=True),
        w_out,
        preferred_element_type=jnp.float32,
    )
    return lax.psum_scatter(partial_terms, "tp", scatter_dimension=1, tiled=True).astype(
        jnp.bfloat16
    )


def solution(mesh):
    return jax.shard_map(
        body,
        mesh=mesh,
        in_specs=(
            P("role", None),
            P(),
            P("role", "tp"),
            P("tp"),
            P("role", None),
            P("role"),
            P("role", None, "tp"),
            P("role", None),
            P("role"),
            P(None, "role", "tp"),
            P(None, "role", "tp"),
            P("tp", "role"),
        ),
        out_specs=P(None, "tp", "role"),
        check_vma=False,
    )
```

profile of v0, /device:TPU:1, one launch (start us, length us, event | category | flops | bytes accessed | tf_op | source)
XLA Modules:
  0.0 328.8 jit_solution(12982000313901675267)
XLA Ops:
  6.5 0.0 copy-start
  6.5 0.0 all-gather.5.cloned.1.call-start
  6.5 0.7 all-gather.5.cloned.1.call-update
  7.3 0.0 all-gather.7.cloned.1.call-start
  7.3 0.7 convert_element_type.55
  8.0 0.7 convert_element_type.57
  8.7 9.5 %fusion = f32[1408]{0:T(1024)S(1)} fusion(bf16[1408,8192]{1,0:T(8,128)(2,1)} %param.12), kind=kLoop, calls=%fused_computation.3 | loop fusion | flops 34601600 | bytes 23074304 | tf_op jit(solution)/shard_map/reduce_sum | solution.py:32
  18.2 0.0 copy-start.6
  18.2 50.8 %all-gather.5.cloned.1.call-done = bf16[8192,256]{1,0:T(8,128)(2,1)} async-done(((bf16[512,256]{1,0:T(8,128)(2,1)}), bf16[8192,256]{1,0:T(8,128)(2,1)}) %all-gather.5.cloned.1.call-update) | async-done | bytes 4194320 | tf_op jit(solution)/shard_map/all_gather | solution.py:36
  69.0 12.8 %fusion.16 = bf16[1408,256]{1,0:T(8,128)(2,1)} fusion(bf16[8192,256]{1,0:T(8,128)(2,1)} %all-gather.5.cloned.1.call-done, bf16[1408,8192]{1,0:T(8,128)(2,1)} %param.12, f32[8192]{0:T(1024)S(1)} %convert_element_type.55, f32[1408]{0:T(1024)S(1)} %add_rsqrt_fusion, f32[256]{0:T(256)S(1)} %convert_element_type.57), kind=kOutput, calls=%fused_computation.22 | convolution fusion | flops 5952438272 | bytes 28023296 | tf_op jit(solution)/shard_map/dot_general | solution.py:35
  81.8 0.0 all-gather.7.cloned.1.call-update
  81.8 0.0 all-gather.9.cloned.1.call-start
  81.9 0.0 copy-done.6
  81.9 0.1 copy.86
  82.0 0.1 reshape.282
  82.1 0.0 copy-done
  82.1 6.8 %gather_fusion = bf16[128,128,256]{2,1,0:T(8,128)(2,1)} fusion(bf16[32,128,256]{2,1,0:T(8,128)(2,1)S(1)} %copy-done, s32[1024]{0:T(1024)S(1)} %pad_clamp_fusion), kind=kCustom, calls=%fused_computation | custom fusion | bytes 16777728 | tf_op jit(solution)/shard_map/gather | solution.py:60
  89.0 0.0 copy-start.7
  89.0 12.7 %reshape.296 = bf16[32,512,1,2,128]{4,3,1,0,2:T(2,128)(2,1)} reshape(bf16[128,128,256]{2,1,0:T(8,128)(2,1)} %gather_fusion) | data formatting | bytes 16777216 | tf_op jit(solution)/shard_map/reshape | solution.py:60
  101.7 0.0 copy-done.4
  101.8 0.0 copy-done.9
  101.8 0.0 copy-done.10
  101.9 20.1 %all-gather = bf16[16,11,2]{1,2,0:T(2,128)(2,1)S(1)} all-gather(bf16[1,11,2]{1,2,0:T(2,128)(2,1)S(1)} %maximum_bitcast_fusion), channel_id=1, replica_groups=mesh['role'=16,'tp'=8] {'role'}, dimensions={0}, use_global_device_ids=true | all-gather | bytes 748 | tf_op jit(solution)/shard_map/all_gather | solution.py:45
  122.0 0.1 copy.93
  122.1 0.1 copy.94
  122.2 0.1 reshape.293
  122.3 0.0 copy-done.5
  122.4 0.0 copy-done.7
  122.4 0.1 iota_compare_fusion
  122.5 0.1 fusion.65
  122.6 0.3 fusion.66
  122.9 0.6 convolution_convert_fusion
  123.5 17.1 %fusion.64 = (bf16[32,512,1,1,128]{4,3,1,0,2:T(2,128)(2,1)S(1)}, bf16[32,512,1,1,128]{4,3,1,0,2:T(2,128)(2,1)}) fusion(bf16[32,512,1,2,128]{4,3,1,0,2:T(2,128)(2,1)} %reshape.296), kind=kLoop, calls=%fused_computation.92 | loop fusion | bytes 16777216 | tf_op jit(solution)/shard_map/slice | solution.py:65
  140.6 2.9 bitcast_reduce_fusion
  143.4 22.7 %all-gather.7.cloned.1.call-done = bf16[176,128,256]{2,1,0:T(8,128)(2,1)} async-done(((bf16[11,128,256]{2,1,0:T(8,128)(2,1)}), bf16[176,128,256]{2,1,0:T(8,128)(2,1)}) %all-gather.7.cloned.1.call-update) | async-done | bytes 11534352 | tf_op jit(solution)/shard_map/all_gather | solution.py:44
  166.2 16.0 %copy.95 = bf16[176,128,256]{1,2,0:T(8,128)(2,1)} copy(bf16[176,128,256]{2,1,0:T(8,128)(2,1)} %all-gather.7.cloned.1.call-done) | data formatting | bytes 23068672 | tf_op jit(solution)/shard_map/all_gather | solution.py:44
  182.1 5.9 %multiply_reduce_fusion = (f32[176,32]{1,0:T(8,128)S(1)}, f32[176,32,128]{2,1,0:T(8,128)}) fusion(bf16[176,128,1,2,128]{1,4,3,0,2:T(8,128)(2,1)} %bitcast.75, bf16[176,32,128]{2,0,1:T(8,128)(2,1)S(1)} %convolution_convert_fusion), kind=kOutput, calls=%fused_computation.21 | convolution fusion | flops 185985536 | bytes 10115072 | tf_op jit(solution)/shard_map/mgqd,mtgd->mgqt/dot_general | solution.py:88
  188.0 0.1 copy.98
  188.1 0.2 select_reduce_fusion.1
  188.3 0.2 select_reduce_fusion
  188.5 0.1 copy.101
  188.6 5.7 %fusion.7 = f32[176,32,128]{2,1,0:T(8,128)S(1)} fusion(bf16[176,128,1,2,128]{1,4,3,0,2:T(8,128)(2,1)} %bitcast.76, f32[176,32,128]{2,1,0:T(8,128)} %get-tuple-element.12, f32[176,32]{1,0:T(8,128)S(1)} %copy.101, pred[176]{0:T(512)(128)(4,1)S(1)} %get-tuple-element.5), kind=kOutput, calls=%fused_computation.10 | convolution fusion | flops 187432960 | bytes 11557040 | tf_op jit(solution)/shard_map/mgqt,mtgd->mgqd/dot_general | solution.py:123
  194.4 0.0 copy-done.2
  194.4 0.0 copy-start.3
  194.4 6.0 %fusion.19 = f32[176,32]{1,0:T(8,128)S(1)} fusion(f32[176,32,128]{2,1,0:T(8,128)S(1)} %copy-done.2, f32[176,32]{1,0:T(8,128)S(1)} %copy.101, pred[176]{0:T(512)(128)(4,1)S(1)} %get-tuple-element.5), kind=kLoop, calls=%fused_computation.23 | loop fusion | flops 2877952 | bytes 2928816 | tf_op jit(solution)/shard_map/reduce_sum | solution.py:109
  200.4 0.0 copy-done.3
  200.4 0.9 fusion.23
  201.3 4.4 %fusion.9 = f32[32,32,128]{2,1,0:T(8,128)S(1)} fusion(bf16[32,512,1,1,128]{4,3,1,0,2:T(2,128)(2,1)} %get-tuple-element.8, f32[32,512,32]{1,2,0:T(8,128)S(1)} %copy-done.3, f32[32,32]{1,0:T(8,128)S(1)} %maximum_maximum_fusion, pred[32,512]{1,0:T(8,128)(4,1)S(1)} %iota_compare_fusion), kind=kOutput, calls=%fused_computation.14 | convolution fusion | flops 136839168 | bytes 6836224 | tf_op jit(solution)/shard_map/rgqt,rtgd->rgqd/dot_general | solution.py:111
  205.7 0.0 copy-start.8
  205.7 2.7 fusion.14
  208.4 0.1 fusion.47
  208.5 0.2 convolution_add_fusion.1
  208.7 0.5 fusion.34
  209.2 0.1 reshape.297
  209.3 0.8 copy.109
  210.1 0.0 all-gather.9.cloned.1.call-update
  210.1 0.0 reduce-scatter.2.cloned.1.call-start
  210.1 53.2 %all-gather.9.cloned.1.call-done = bf16[4,512,1024]{2,1,0:T(8,128)(2,1)} async-done(((bf16[4,32,1024]{2,1,0:T(8,128)(2,1)}), bf16[4,512,1024]{2,1,0:T(8,128)(2,1)}) %all-gather.9.cloned.1.call-update) | async-done | bytes 4194320 | tf_op jit(solution)/shard_map/all_gather | solution.py:137
  263.3 0.0 copy-done.8
  263.3 6.6 %fusion.37 = f32[4,512,512]{2,1,0:T(8,128)} fusion(bf16[4,512,1024]{2,1,0:T(8,128)(2,1)} %all-gather.9.cloned.1.call-done, bf16[1024,512]{1,0:T(8,128)(2,1)S(1)} %copy-done.8), kind=kOutput, calls=%fused_computation.46 | convolution fusion | flops 2147483648 | bytes 9437184 | tf_op jit(solution)/shard_map/srk,kc->src/dot_general | solution.py:135
  269.9 0.0 reduce-scatter.2.cloned.1.call-update
  270.0 50.5 %reduce-scatter.2.cloned.1.call-done = f32[4,64,512]{2,1,0:T(8,128)} async-done(((f32[4,512,512]{2,1,0:T(8,128)}), f32[4,64,512]{2,1,0:T(8,128)}) %reduce-scatter.2.cloned.1.call-update) | async-done | bytes 524304 | tf_op jit(solution)/shard_map/reduce_scatter | solution.py:141
  320.5 1.8 convert_element_type.66
  322.2 0.0 copy-done.1
  (21 shorter events, 0.2 us)
Async XLA Ops:
  6.5 75.6 %copy-start = (bf16[32,128,256]{2,1,0:T(8,128)(2,1)S(1)}, bf16[32,128,256]{2,1,0:T(8,128)(2,1)}, u32[]{:S(2)}) copy-start(bf16[32,128,256]{2,1,0:T(8,128)(2,1)} %param.18) | copy-start | bytes 6291460
  6.5 62.4 %all-gather.5.cloned.1.call-start = ((), (), s32[]{:S(2)}) async-start(), calls=%async_computation.1 | async-start | bytes 4456448 | tf_op jit(solution)/shard_map/all_gather | solution.py:36
  7.3 158.9 %all-gather.7.cloned.1.call-start = ((), (), s32[]{:S(2)}) async-start(), calls=%async_computation.2 | async-start | bytes 12255232 | tf_op jit(solution)/shard_map/all_gather | solution.py:44
  18.2 63.7 %copy-start.6 = (s32[32,4]{0,1:T(4,128)S(1)}, s32[32,4]{0,1:T(4,128)}, u32[]{:S(2)}) copy-start(s32[32,4]{0,1:T(4,128)} %param.19) | copy-start | bytes 1540
  81.8 181.5 %all-gather.9.cloned.1.call-start = ((), (), s32[]{:S(2)}) async-start(), calls=%async_computation.3 | async-start | bytes 4456448 | tf_op jit(solution)/shard_map/all_gather | solution.py:137
  88.9 12.8 %copy-start.4 = (bf16[4,32,1024]{2,1,0:T(8,128)(2,1)S(1)}, bf16[4,32,1024]{2,1,0:T(8,128)(2,1)}, u32[]{:S(2)}) copy-start(bf16[4,32,1024]{2,1,0:T(8,128)(2,1)} %param.21) | copy-start | bytes 786436
  88.9 12.9 %copy-start.9 = (s32[11,1]{0,1:T(1,128)S(1)}, s32[11,1]{0,1:T(1,128)}, u32[]{:S(2)}) copy-start(s32[11,1]{0,1:T(1,128)} %param.16) | copy-start | bytes 136
  88.9 12.9 %copy-start.10 = (s32[11]{0:T(128)S(1)}, s32[11]{0:T(128)}, u32[]{:S(2)}) copy-start(s32[11]{0:T(128)} %param.17) | copy-start | bytes 136
  89.0 33.4 %copy-start.5 = (bf16[4,32,256]{2,1,0:T(8,128)(2,1)S(1)}, bf16[4,32,256]{2,1,0:T(8,128)(2,1)}, u32[]{:S(2)}) copy-start(bf16[4,32,256]{2,1,0:T(8,128)(2,1)} %param.22) | copy-start | bytes 196612
  89.0 33.5 %copy-start.7 = (s32[32]{0:T(128)S(1)}, s32[32]{0:T(128)}, u32[]{:S(2)}) copy-start(s32[32]{0:T(128)} %param.20) | copy-start | bytes 388
  188.6 5.8 %copy-start.2 = (f32[176,32,128]{2,1,0:T(8,128)S(1)}, f32[176,32,128]{2,1,0:T(8,128)}, u32[]{:S(2)}) copy-start(f32[176,32,128]{2,1,0:T(8,128)} %get-tuple-element.12) | copy-start | bytes 8650756
  194.4 6.0 %copy-start.3 = (f32[32,512,32]{1,2,0:T(8,128)S(1)}, f32[32,512,32]{1,2,0:T(8,128)}, u32[]{:S(2)}) copy-start(f32[32,512,32]{1,2,0:T(8,128)} %get-tuple-element.14) | copy-start | bytes 6291460
  205.7 57.6 %copy-start.8 = (bf16[1024,512]{1,0:T(8,128)(2,1)S(1)}, bf16[1024,512]{1,0:T(8,128)(2,1)}, u32[]{:S(2)}) copy-start(bf16[1024,512]{1,0:T(8,128)(2,1)} %param.23) | copy-start | bytes 3145732
  210.1 110.4 %reduce-scatter.2.cloned.1.call-start = ((), (), s32[]{:S(2)}) async-start(), calls=%async_computation.4 | async-start | bytes 4718592 | tf_op jit(solution)/shard_map/reduce_scatter | solution.py:141
  263.3 58.9 %copy-start.1 = (bf16[32,128,256]{2,1,0:T(8,128)(2,1)S(1)}, bf16[32,128,256]{2,1,0:T(8,128)(2,1)}, u32[]{:S(2)}) copy-start(bf16[32,128,256]{2,1,0:T(8,128)(2,1)} %param.18) | copy-start | bytes 6291460
Sparse Core Ops, SparseCore 0:
  9.8 59.0 all-gather.4
  82.0 84.1 all-gather.6
  210.2 53.0 all-gather.8
  270.1 50.3 reduce-scatter.1
where the time goes:
time: 330 us; the launch traced here: 329 us
  waiting for transfers between devices  178 us (54%)
  local copies, waits for them, and re-layouts  54.3 us (16%)
  matrix products  42.6 us (13%)
  other arithmetic  20.1 us (6%)
  blocking collectives  20.1 us (6%)
  between operations  13.4 us (4%)
    all_gather x1, waiting for transfers between devices, body(): lax.all_gather(attended, 'role', axis=1, tiled=True)  53.2 us
    all_gather x1, waiting for transfers between devices, body(): lax.all_gather(w_kv, 'role', axis=0, tiled=True)  50.8 us
    reduce_scatter x1, waiting for transfers between devices, body(): lax.psum_scatter(partial_terms, 'tp', scatter_dimension=1, tiled=True)  50.5 us
    all_gather x1, waiting for transfers between devices, body(): lax.all_gather(page_blocks, 'role', axis=0, tiled=True)  22.7 us
    all_gather x1, blocking collectives, body(): lax.all_gather(tags, 'role', axis=0, tiled=True)  20.1 us
    slice x1, local copies, waits for them, and re-layouts, body(): cache_kv[:, :, :, 0]  17.1 us
    all_gather x1, local copies, waits for them, and re-layouts, body(): lax.all_gather(page_blocks, 'role', axis=0, tiled=True)  16 us
    dot_general x1, matrix products, body(): jnp.dot(normed, lax.all_gather(w_kv, 'role', axis=0, tiled=True), preferr...  12.8 us
  transfers between devices with their start and end apart: 4, of which 4 were waited for; matrix products, arithmetic and copies ran while one was open for 16% of the time, Pallas kernels for 0%

commit v1 on v0

v1 whole, which is shorter than its diff:
```python
import functools
import math

import jax
import jax.numpy as jnp
from jax import lax
from jax.experimental import pallas as pl
from jax.experimental.pallas import tpu as pltpu
from jax.sharding import PartitionSpec as P

HS = 128
PAGE = 128
EPSILON = 1e-06
LOW = -1e30
MESH = pl.DeviceIdType.MESH
BF = jnp.bfloat16
F32 = jnp.float32

NR = 16
NT = 8
NP = 11
RQ = 32
STEPS = 4
PER = 8
KB = 512
KVW = 256
ROWS = NP * PAGE
TILE = 352
NOUT = 512
SCALING = 1.0 / math.sqrt(HS)
NT_DIMS = (((1,), (1,)), ((), ()))


def kernel(
    x_hbm,
    w_hbm,
    bias_ref,
    owner_ref,
    req_ref,
    kv_hbm,
    bt_ref,
    len_ref,
    dq_hbm,
    dkv_hbm,
    wout_hbm,
    out_ref,
    xv,
    wv,
    kv,
    dq,
    dkv,
    wout,
    acc,
    sq,
    qf,
    qb,
    ac,
    lc,
    vtag,
    rtag,
    tvec,
    tsm,
    slot_of,
    page_of,
    qs,
    qr,
    pacc,
    accs,
    racc,
    sst,
    rst,
    lt,
    sb,
    aall,
    ps,
    pr,
    x_sem,
    in_sem,
    t_sem,
    w_ss,
    w_rs,
    wf_ss,
    tag_ss,
    tag_rs,
    q_ss,
    q_rs,
    a_ss,
    a_rs,
    l_ss,
    l_rs,
    g_ss,
    g_rs,
    gf_ss,
    p_ss,
    p_rs,
):
    me = lax.axis_index("role")
    tp = lax.axis_index("tp")
    chip, core = me // 2, me % 2
    z, yh = chip // 2, chip % 2
    sib = 2 * chip + (1 - core)

    def to_chip(d, sign):
        dz, dy = d // 2, d % 2
        return ((z + sign * dz + 4) % 4) * 2 + (yh + dy) % 2

    def rc(src, dst, ss, rs, role, t=None):
        return pltpu.make_async_remote_copy(
            src_ref=src,
            dst_ref=dst,
            send_sem=ss,
            recv_sem=rs,
            device_id=(role, tp if t is None else t),
            device_id_type=MESH,
        )

    def x_copy(c):
        return pltpu.make_async_copy(x_hbm.at[:, pl.ds(pl.multiple_of(c * KB, KB), KB)], xv.at[c], x_sem.at[c])

    own_w = pltpu.make_async_copy(w_hbm, wv.at[me], in_sem.at[0])
    kv_c = pltpu.make_async_copy(kv_hbm, kv, in_sem.at[1])
    dq_c = pltpu.make_async_copy(dq_hbm, dq, in_sem.at[2])
    dkv_c = pltpu.make_async_copy(dkv_hbm, dkv, in_sem.at[3])
    wout_c = pltpu.make_async_copy(wout_hbm, wout, in_sem.at[4])
    own_w.start()
    dq_c.start()
    dkv_c.start()
    kv_c.start()

    barrier = pltpu.get_barrier_semaphore()

    def greet_role(d, _):
        pl.semaphore_signal(barrier, inc=1, device_id=((me + d) % NR, tp), device_id_type=MESH)
        return 0

    def greet_tp(d, _):
        pl.semaphore_signal(barrier, inc=1, device_id=(me, (tp + d) % NT), device_id_type=MESH)
        return 0

    lax.fori_loop(1, NR, greet_role, 0)
    lax.fori_loop(1, NT, greet_tp, 0)

    lane = lax.broadcasted_iota(jnp.int32, (8, 128), 1)
    owners = [owner_ref[i] for i in range(NP)]
    tags = jnp.full((8, 128), -1, jnp.int32)
    slots = []
    for i in range(NP):
        rank = jnp.int32(0)
        for j in range(i):
            rank = rank + (owners[j] == owners[i]).astype(jnp.int32)
        slot = 2 * owners[i] + rank
        slots.append(slot)
        slot_of[i] = slot
        tags = jnp.where(lane == slot, req_ref[i], tags)
    vtag[...] = tags
    rtag[me] = tags

    own_w.wait()
    pl.semaphore_wait(barrier, NR - 1 + NT - 1)

    def send_tag(d, _):
        p = (me + d) % NR
        rc(vtag, rtag.at[me], tag_ss.at[d], tag_rs.at[me], p).start()
        return 0

    lax.fori_loop(1, NR, send_tag, 0)

    def w_send(d):
        return rc(wv.at[me], wv.at[me], w_ss.at[d], w_rs.at[me], 2 * to_chip(d, 1) + core)

    w_sib = rc(wv.at[me], wv.at[me], w_ss.at[0], w_rs.at[me], sib)
    w_sib.start()

    def start_w(d, _):
        w_send(d).start()
        return 0

    lax.fori_loop(1, 8, start_w, 0)

    x_copy(me).start()
    x_copy(sib).start()

    def start_x(d, _):
        c = to_chip(d, -1)
        x_copy(2 * c + core).start()
        x_copy(2 * c + (1 - core)).start()
        return 0

    lax.fori_loop(1, 8, start_x, 0)
    wout_c.start()

    dq_c.wait()
    for s in range(STEPS):
        for h in range(PER):
            qf[pl.ds(s * PER + h, RQ, stride=RQ), :] = dq[s, :, h * HS : (h + 1) * HS].astype(F32)

    def find_page(s, _):
        i = jnp.int32(0)
        for j in range(NP):
            i = jnp.where(slots[j] == s, j, i)
        page_of[s] = i
        return 0

    lax.fori_loop(0, 2 * NR, find_page, 0)

    acc[...] = jnp.zeros_like(acc)
    sq[...] = jnp.zeros_like(sq)

    dkv_c.wait()
    kv_c.wait()

    def attend(r, _):
        q = qf[pl.ds(pl.multiple_of(r * RQ, RQ), RQ), :].astype(BF)
        qb[r] = q
        pages = [kv[bt_ref[r * 4 + j]] for j in range(4)]
        own = dkv[...]
        keys = jnp.concatenate([p[:, :HS] for p in pages], axis=0)
        values = jnp.concatenate([p[:, HS:] for p in pages], axis=0)
        s1 = lax.dot_general(q, keys, NT_DIMS, preferred_element_type=F32) * SCALING
        s2 = lax.dot_general(q, own[:, :HS], NT_DIMS, preferred_element_type=F32) * SCALING
        col = lax.broadcasted_iota(jnp.int32, s1.shape, 1)
        s1 = jnp.where(col < len_ref[r], s1, LOW)
        col2 = lax.broadcasted_iota(jnp.int32, s2.shape, 1)
        row2 = lax.broadcasted_iota(jnp.int32, s2.shape, 0)
        s2 = jnp.where((col2 % RQ == r) & (col2 // RQ <= row2 // PER), s2, LOW)
        top = jnp.maximum(jnp.max(s1, axis=1, keepdims=True), jnp.max(s2, axis=1, keepdims=True))
        p1 = jnp.exp(s1 - top)
        p2 = jnp.exp(s2 - top)
        total = jnp.sum(p1, axis=1, keepdims=True) + jnp.sum(p2, axis=1, keepdims=True)
        o = jnp.dot(p1.astype(BF), values, preferred_element_type=F32)
        o = o + jnp.dot(p2.astype(BF), own[:, HS:], preferred_element_type=F32)
        ac[pl.ds(r, RQ, stride=RQ), :] = o / total
        lc[pl.ds(r, RQ, stride=RQ), :] = jnp.broadcast_to(top + jnp.log(total), (RQ, HS))
        return 0

    lax.fori_loop(0, RQ, attend, 0)

    tmat = jnp.full((8, 128), -1, jnp.int32)

    def wait_tag(d, t):
        p = (me - d + NR) % NR

        @pl.when(d > 0)
        def _():
            rc(vtag, rtag.at[p], tag_ss.at[0], tag_rs.at[p], p).wait_recv()

        moved = pltpu.roll(rtag[p], (2 * p - 2 * me + 128) % 128, 1)
        return jnp.where(lane // 2 == p, moved, t)

    tmat = lax.fori_loop(0, NR, wait_tag, tmat)
    tvec[...] = tmat
    t_c = pltpu.make_async_copy(tvec, tsm, t_sem)
    t_c.start()
    t_c.wait()

    def pick(s, _):
        qs[s] = qb[jnp.maximum(tsm[0, s], 0)]
        return 0

    lax.fori_loop(0, 2 * NR, pick, 0)

    def send_q(d, _):
        p = (me + d) % NR
        rc(qs.at[pl.ds(2 * p, 2)], qr.at[pl.ds(2 * me, 2)], q_ss.at[d], q_rs.at[me], p).start()
        return 0

    lax.fori_loop(1, NR, send_q, 0)
    qr[pl.ds(2 * me, 2)] = qs[pl.ds(2 * me, 2)]

    def project(c):
        x_copy(c).wait()

        def tile(t, _):
            rows = pl.ds(pl.multiple_of(t * TILE, TILE), TILE)
            xa = xv[c, rows, :]
            acc[rows, :] += jnp.dot(xa, wv[c], preferred_element_type=F32)
            xf = xa.astype(F32)
            xx = xf * xf
            sq[rows, :] += (xx[:, :128] + xx[:, 128:256]) + (xx[:, 256:384] + xx[:, 384:])
            return 0

        lax.fori_loop(0, ROWS // TILE, tile, 0)

    def w_recv(p):
        rc(wv.at[p], wv.at[p], w_ss.at[0], w_rs.at[p], sib).wait_recv()

    def w_fwd(d, p):
        return rc(wv.at[p], wv.at[p], wf_ss.at[d], w_rs.at[p], sib)

    project(me)
    w_recv(sib)
    project(sib)

    def arrive(d, _):
        c = to_chip(d, -1)
        w_recv(2 * c + core)
        w_fwd(d, 2 * c + core).start()
        project(2 * c + core)
        w_recv(2 * c + (1 - core))
        project(2 * c + (1 - core))
        return 0

    lax.fori_loop(1, 8, arrive, 0)

    def wait_q(d, _):
        p = (me - d + NR) % NR
        rc(qs.at[pl.ds(0, 2)], qr.at[pl.ds(2 * p, 2)], q_ss.at[0], q_rs.at[p], p).wait_recv()
        return 0

    lax.fori_loop(1, NR, wait_q, 0)
    bias = bias_ref[...].astype(F32)
    lane_k = lax.broadcasted_iota(jnp.int32, (RQ, 128), 1)

    def page(i, st):
        rows = pl.ds(pl.multiple_of(i * PAGE, PAGE), PAGE)
        inverse = lax.rsqrt(jnp.sum(sq[rows, :], axis=1, keepdims=True) * (1.0 / (NR * KB)) + EPSILON)
        f = (acc[rows, :] * inverse + bias).astype(BF)
        slot = slot_of[i]
        q = qr[slot]
        s = lax.dot_general(q, f[:, :HS], NT_DIMS, preferred_element_type=F32) * SCALING
        top = jnp.max(s, axis=1, keepdims=True)
        p = jnp.exp(s - top)
        total = jnp.sum(p, axis=1, keepdims=True)
        o = jnp.dot(p.astype(BF), f[:, HS:], preferred_element_type=F32) / total
        pacc[i] = o.astype(BF)
        return jnp.where(lane_k == slot, top + jnp.log(total), st)

    st = lax.fori_loop(0, NP, page, jnp.full((RQ, 128), LOW, F32))
    packed = st[0:8]
    for a in range(1, 4):
        packed = jnp.where(lane // 32 == a, pltpu.roll(st[8 * a : 8 * a + 8], 32 * a, 1), packed)
    sst[...] = packed
    rst[me] = packed

    def place(s, _):
        accs[s] = pacc[page_of[s]]
        return 0

    lax.fori_loop(0, 2 * NR, place, 0)

    def send_acc(d, _):
        p = (me + d) % NR
        rc(accs.at[pl.ds(2 * p, 2)], racc.at[pl.ds(2 * me, 2)], a_ss.at[d], a_rs.at[me], p).start()
        rc(sst, rst.at[me], l_ss.at[d], l_rs.at[me], p).start()
        return 0

    lax.fori_loop(1, NR, send_acc, 0)
    racc[pl.ds(2 * me, 2)] = accs[pl.ds(2 * me, 2)]

    lt[...] = jnp.full((RQ, 128), LOW, F32)

    def take(d, _):
        p = (me - d + NR) % NR

        @pl.when(d > 0)
        def _():
            rc(sst, rst.at[p], l_ss.at[0], l_rs.at[p], p).wait_recv()
            rc(accs.at[pl.ds(0, 2)], racc.at[pl.ds(2 * p, 2)], a_ss.at[0], a_rs.at[p], p).wait_recv()

        got = rst[p]
        for a in range(4):
            moved = pltpu.roll(got, (2 * p - 2 * me - 32 * a + 256) % 128, 1)
            lt[8 * a : 8 * a + 8, :] = jnp.where(lane // 2 == p, moved, lt[8 * a : 8 * a + 8, :])
        for c in range(2):
            sb[pl.ds(2 * p + c, RQ, stride=RQ), :] = racc[2 * p + c].astype(F32)
        return 0

    lax.fori_loop(0, NR, take, 0)

    mine = jnp.broadcast_to(tvec[0:1, :], (RQ, 128)) == lax.broadcasted_iota(jnp.int32, (RQ, 128), 0)

    def g_send(s, d):
        role = jnp.where(d == 0, sib, 2 * to_chip(d, 1) + core)
        return rc(aall.at[s, me], aall.at[s, me], g_ss.at[s, d], g_rs.at[s, me], role)

    def merge(s, _):
        for h in range(PER):
            k = s * PER + h
            rows = pl.ds(pl.multiple_of(k * RQ, RQ), RQ)
            scores = jnp.where(mine, jnp.broadcast_to(lt[pl.ds(k, 1), :], (RQ, 128)), LOW)
            base = lc[rows, :]
            top = jnp.maximum(jnp.max(scores, axis=1, keepdims=True), base)
            e = jnp.exp(scores - top)
            wc = jnp.exp(base - top)
            total = wc + jnp.sum(e, axis=1, keepdims=True)
            pv = jnp.dot(e[:, : 2 * NR].astype(BF), sb[rows, :].astype(BF), preferred_element_type=F32)
            merged = (wc * ac[rows, :] + pv) / total
            aall[s, me, :, h * HS : (h + 1) * HS] = merged.astype(BF)

        def start_g(d, _):
            g_send(s, d).start()
            return 0

        lax.fori_loop(0, 8, start_g, 0)
        return 0

    lax.fori_loop(0, STEPS, merge, 0)
    wout_c.wait()

    def g_recv(s, p):
        rc(aall.at[s, p], aall.at[s, p], g_ss.at[s, 0], g_rs.at[s, p], sib).wait_recv()

    def g_fwd(s, d, p):
        return rc(aall.at[s, p], aall.at[s, p], gf_ss.at[s, d], g_rs.at[s, p], sib)

    def p_send(s, d):
        t = (tp + d) % NT
        return rc(ps.at[s, t], pr.at[tp, s], p_ss.at[s, d], p_rs.at[s, tp], me, t)

    def finish(s, _):
        def pass_on(d, _):
            p = 2 * to_chip(d, -1) + core
            g_recv(s, p)
            g_fwd(s, d, p).start()
            return 0

        lax.fori_loop(1, 8, pass_on, 0)
        g_recv(s, sib)

        def other(d, _):
            g_recv(s, 2 * to_chip(d, -1) + (1 - core))
            return 0

        lax.fori_loop(1, 8, other, 0)

        def part(j, _):
            a = aall[s, pl.ds(j * 8, 8)].reshape(8 * RQ, 1024)
            o = jnp.dot(a, wout[...], preferred_element_type=F32).astype(BF)
            ps[s, pl.ds(j * 4, 4)] = o.reshape(4, 2 * RQ, NOUT)
            return 0

        lax.fori_loop(0, 2, part, 0)

        def start_p(d, _):
            p_send(s, d).start()
            return 0

        lax.fori_loop(1, NT, start_p, 0)
        return 0

    lax.fori_loop(0, STEPS, finish, 0)

    def total_of(s, _):
        def add(d, o):
            t = (tp - d + NT) % NT
            rc(ps.at[s, 0], pr.at[t, s], p_ss.at[s, 0], p_rs.at[s, t], me, t).wait_recv()
            return o

        lax.fori_loop(1, NT, add, 0)
        o = ps[s, tp].astype(F32)
        for d in range(1, NT):
            o = o + pr[(tp + d) % NT, s].astype(F32)
        out_ref[s] = o.astype(BF)
        return 0

    lax.fori_loop(0, STEPS, total_of, 0)

    def drain(d, _):
        rc(vtag, rtag.at[me], tag_ss.at[d], tag_rs.at[me], sib).wait_send()
        rc(qs.at[pl.ds(0, 2)], qr.at[pl.ds(0, 2)], q_ss.at[d], q_rs.at[me], sib).wait_send()
        rc(accs.at[pl.ds(0, 2)], racc.at[pl.ds(0, 2)], a_ss.at[d], a_rs.at[me], sib).wait_send()
        rc(sst, rst.at[me], l_ss.at[d], l_rs.at[me], sib).wait_send()
        return 0

    lax.fori_loop(1, NR, drain, 0)
    w_sib.wait_send()

    def drain_w(d, _):
        w_send(d).wait_send()
        w_fwd(d, me).wait_send()
        return 0

    lax.fori_loop(1, 8, drain_w, 0)

    def drain_g(s, _):
        def one(d, _):
            g_send(s, d).wait_send()

            @pl.when(d > 0)
            def _():
                g_fwd(s, d, me).wait_send()
                p_send(s, d).wait_send()

            return 0

        lax.fori_loop(0, 8, one, 0)
        return 0

    lax.fori_loop(0, STEPS, drain_g, 0)


def body(
    x_pre,
    ln_gain,
    w_kv,
    kv_bias,
    page_owner,
    page_req,
    kv_pool,
    block_table,
    cache_len,
    dec_q,
    dec_kv,
    w_out,
):
    gain = lax.dynamic_slice_in_dim(ln_gain, lax.axis_index("role") * KB, KB, 0)
    scaled = (w_kv.astype(F32) * gain.astype(F32)[:, None]).astype(BF)
    any_spec = pl.BlockSpec(memory_space=pl.ANY)
    smem = pl.BlockSpec(memory_space=pltpu.SMEM)
    vmem = pl.BlockSpec(memory_space=pltpu.VMEM)
    dma = pltpu.SemaphoreType.DMA
    V = pltpu.VMEM
    scratch = [
        V((NR, ROWS, KB), BF),
        V((NR, KB, KVW), BF),
        V((32, PAGE, KVW), BF),
        V((STEPS, RQ, 1024), BF),
        V((STEPS * RQ, KVW), BF),
        V((1024, NOUT), BF),
        V((ROWS, KVW), F32),
        V((ROWS, 128), F32),
        V((RQ * RQ, HS), F32),
        V((RQ, RQ, HS), BF),
        V((RQ * RQ, HS), F32),
        V((RQ * RQ, HS), F32),
        V((8, 128), jnp.int32),
        V((NR, 8, 128), jnp.int32),
        V((8, 128), jnp.int32),
        pltpu.SMEM((8, 128), jnp.int32),
        pltpu.SMEM((16,), jnp.int32),
        pltpu.SMEM((2 * NR,), jnp.int32),
        V((2 * NR, RQ, HS), BF),
        V((2 * NR, RQ, HS), BF),
        V((NP, RQ, HS), BF),
        V((2 * NR, RQ, HS), BF),
        V((2 * NR, RQ, HS), BF),
        V((8, 128), F32),
        V((NR, 8, 128), F32),
        V((RQ, 128), F32),
        V((RQ * RQ, HS), F32),
        V((STEPS, NR, RQ, 1024), BF),
        V((STEPS, NT, 2 * RQ, NOUT), BF),
        V((NT, STEPS, 2 * RQ, NOUT), BF),
        dma((NR,)),
        dma((5,)),
        dma,
        dma((8,)),
        dma((NR,)),
        dma((8,)),
        dma((NR,)),
        dma((NR,)),
        dma((NR,)),
        dma((NR,)),
        dma((NR,)),
        dma((NR,)),
        dma((NR,)),
        dma((NR,)),
        dma((STEPS, 8)),
        dma((STEPS, NR)),
        dma((STEPS, 8)),
        dma((STEPS, 8)),
        dma((STEPS, NT)),
    ]
    return pl.pallas_call(
        kernel,
        out_shape=jax.ShapeDtypeStruct((STEPS, 2 * RQ, NOUT), BF),
        in_specs=[any_spec, any_spec, vmem, smem, smem, any_spec, smem, smem, any_spec, any_spec, any_spec],
        out_specs=vmem,
        scratch_shapes=scratch,
        compiler_params=pltpu.CompilerParams(
            collective_id=0, has_side_effects=True, vmem_limit_bytes=58 * 1024 * 1024
        ),
    )(
        x_pre,
        scaled,
        kv_bias.reshape(1, KVW),
        page_owner.reshape(NP),
        page_req,
        kv_pool,
        block_table.reshape(RQ * 4),
        cache_len,
        dec_q,
        dec_kv.reshape(STEPS * RQ, KVW),
        w_out,
    )


def solution(mesh):
    return jax.shard_map(
        body,
        mesh=mesh,
        in_specs=(
            P("role", None),
            P(),
            P("role", "tp"),
            P("tp"),
            P("role", None),
            P("role"),
            P("role", None, "tp"),
            P("role", None),
            P("role"),
            P(None, "role", "tp"),
            P(None, "role", "tp"),
            P("tp", "role"),
        ),
        out_specs=P(None, "tp", "role"),
        check_vma=False,
    )
```

time: 330 us -> 117 us (0.35)
  waiting for transfers between devices: 178 us -> 0 us
  Pallas kernels: 0 us -> 110 us
  local copies, waits for them, and re-layouts: 54.3 us -> 4.3 us
  matrix products: 42.6 us -> 0 us
  blocking collectives: 20.1 us -> 0 us
  other arithmetic: 20.1 us -> 2.54 us
  between operations: 13.4 us -> 0.01 us
    all_gather x3 -> x0, waiting for transfers between devices: 127 us -> none  [the longest x1 53.2 us: body(): lax.all_gather(attended, 'role', axis=1, tiled=True)]
    pallas_call x0 -> x1, Pallas kernels: none -> 110 us  [body(): pl.pallas_call(kernel, out_shape=jax.ShapeDtypeStruct((STEPS, 2 * RQ, NOU...]
    reduce_scatter x1 -> x0, waiting for transfers between devices: 50.5 us -> none  [body(): lax.psum_scatter(partial_terms, 'tp', scatter_dimension=1, tiled=True)]
    dot_general x11 -> x0, matrix products: 42.6 us -> none  [the longest x1 12.8 us: body(): jnp.dot(normed, lax.all_gather(w_kv, 'role', axis=0, tiled=True), preferr...]
    all_gather x1 -> x0, blocking collectives: 20.1 us -> none  [body(): lax.all_gather(tags, 'role', axis=0, tiled=True)]
    slice x2 -> x0, local copies, waits for them, and re-layouts: 17.2 us -> none  [the longest x1 17.1 us: body(): cache_kv[:, :, :, 0]]
    reduce_sum x5 -> x0, other arithmetic: 16.6 us -> none  [the longest x1 9.45 us: body(): jnp.mean(activations * activations, axis=-1, keepdims=True) + EPSILON]
    all_gather x2 -> x0, local copies, waits for them, and re-layouts: 16.1 us -> none  [the longest x1 16 us: body(): lax.all_gather(page_blocks, 'role', axis=0, tiled=True)]
  transfers between devices with their start and end apart: 4 -> 0, of which waited for: 4 -> 0; matrix products, arithmetic and copies ran while one was open for 16% -> 0% of each run, Pallas kernels for 0% -> 0%
where the time goes in v1:
time: 117 us
  Pallas kernels  110 us (94%)
  local copies, waits for them, and re-layouts  4.3 us (4%)
  other arithmetic  2.54 us (2%)
    pallas_call x1, Pallas kernels, body(): pl.pallas_call(kernel, out_shape=jax.ShapeDtypeStruct((STEPS, 2 * RQ, NOU...  110 us
    convert_element_type x2, other arithmetic, body(): scaled = (w_kv.astype(F32) * gain.astype(F32)[:, None]).astype(BF)  2.54 us
    unnamed x2, local copies, waits for them, and re-layouts  2.43 us

profile of v1, /device:TPU:1, one launch (start us, length us, event | category | flops | bytes accessed | tf_op | source)
XLA Modules:
  0.0 116.6 jit_solution(12882385690487123327)
XLA Ops:
  0.0 1.2 %reshape.13.bias_ref = bf16[1,256]{1,0:T(2,128)(2,1)} reshape(bf16[256]{0:T(256)(128)(2,1)} %param.15) | data formatting | bytes 1024 | tf_op jit(solution)/shard_map/reshape | solution.py:576
  1.2 0.8 dynamic-slice_convert_fusion
  2.0 0.8 copy.14
  2.7 0.6 reshape.15.bt_ref
  3.4 1.8 %multiply_convert_fusion.w_hbm = bf16[512,256]{1,0:T(8,128)(2,1)} fusion(bf16[512,256]{1,0:T(8,128)(2,1)} %param.14, f32[512]{0:T(512)S(1)} %dynamic-slice_convert_fusion), kind=kLoop, calls=%fused_computation | loop fusion | flops 393216 | bytes 526336 | tf_op jit(solution)/shard_map/convert_element_type | solution.py:507
  5.2 109.8 %shard_map.118 = bf16[4,64,512]{2,1,0:T(8,128)(2,1)} custom-call(bf16[1408,8192]{1,0:T(8,128)(2,1)} %x_hbm.1, bf16[512,256]{1,0:T(8,128)(2,1)} %multiply_convert_fusion.w_hbm, bf16[1,256]{1,0:T(2,128)(2,1)} %reshape.13.bias_ref, s32[11]{0:T(128)} %bitcast.3, s32[11]{0:T(128)} %req_ref.1, bf16[32,128,256]{2,1,0:T(8,128)(2,1)} %kv_hbm.1, s32[128]{0:T(128)} %reshape.15.bt_ref, ...), custom_call_target="tpu_custom_call" | custom-call | tf_op jit(solution)/shard_map/pallas_call | solution.py:564
  114.9 1.7 %copy.16 = bf16[4,64,512]{2,1,0:T(8,128)(2,1)} copy(bf16[4,64,512]{2,1,0:T(8,128)(2,1)} %shard_map.118) | data formatting | bytes 524288

commit v2 on v1

v2 whole, which is shorter than its diff:
```python
import functools
import math

import jax
import jax.numpy as jnp
from jax import lax
from jax.experimental import pallas as pl
from jax.experimental.pallas import tpu as pltpu
from jax.sharding import PartitionSpec as P

HS = 128
PAGE = 128
EPSILON = 1e-06
LOW = -1e30
MESH = pl.DeviceIdType.MESH
BF = jnp.bfloat16
F32 = jnp.float32

NR = 16
NT = 8
NP = 11
RQ = 32
STEPS = 4
PER = 8
KB = 512
KVW = 256
ROWS = NP * PAGE
TILE = 352
UNROLL = 2
NOUT = 512
SCALING = 1.0 / math.sqrt(HS)
NT_DIMS = (((1,), (1,)), ((), ()))


def kernel(
    x_hbm,
    gain_ref,
    w_hbm,
    bias_ref,
    owner_ref,
    req_ref,
    kv_hbm,
    bt_ref,
    len_ref,
    dq_hbm,
    dkv_hbm,
    wout_hbm,
    out_ref,
    xv,
    wraw,
    wv,
    kv,
    dq,
    dkv,
    wout,
    acc,
    sq,
    qf,
    qb,
    ac,
    lc,
    vtag,
    rtag,
    tvec,
    tsm,
    slot_of,
    page_of,
    qs,
    qr,
    pacc,
    accs,
    racc,
    sst,
    rst,
    lt,
    sb,
    aall,
    ps,
    px,
    ys,
    py,
    ko,
    x_sem,
    in_sem,
    t_sem,
    w_ss,
    w_rs,
    tag_ss,
    tag_rs,
    q_ss,
    q_rs,
    a_ss,
    a_rs,
    l_ss,
    l_rs,
    g_ss,
    g_rs,
    p_ss,
    p_rs,
    y_ss,
    y_rs,
):
    me = lax.axis_index("role")
    tp = lax.axis_index("tp")
    chip, core = me // 2, me % 2
    z, yh = chip // 2, chip % 2
    yl, xx = tp // 4, tp % 4
    sib = 2 * chip + (1 - core)

    def chip_at(dz, dy):
        return ((z + dz) % 4) * 2 + (yh + dy) % 2

    c_y, c_p, c_m, c_2 = chip_at(0, 1), chip_at(1, 0), chip_at(3, 0), chip_at(2, 0)
    c_yp, c_ym, c_y2 = chip_at(1, 1), chip_at(3, 1), chip_at(2, 1)

    def rc(src, dst, ss, rs, role, t=None):
        return pltpu.make_async_remote_copy(
            src_ref=src,
            dst_ref=dst,
            send_sem=ss,
            recv_sem=rs,
            device_id=(role, tp if t is None else t),
            device_id_type=MESH,
        )

    class Gather:
        def __init__(self, block, ss, rs):
            self.block, self.ss, self.rs = block, ss, rs

        def copy(self, i, of, to):
            return rc(self.block(of), self.block(of), self.ss(i), self.rs(of), to)

        def ops(self):
            ch = lambda c: 2 * c + core
            return [
                (me, ch(c_y)),
                (me, ch(c_p)),
                (me, ch(c_m)),
                (me, ch(c_2)),
                (me, sib),
                (ch(c_y), ch(c_p)),
                (ch(c_y), ch(c_m)),
                (ch(c_2), ch(c_y)),
            ] + [(ch(c), sib) for c in (c_p, c_m, c_y, c_2, c_yp, c_ym, c_y2)]

        def start(self, *which):
            ops = self.ops()
            for i in which:
                self.copy(i, *ops[i]).start()

        def wait(self, role):
            self.copy(0, role, sib).wait_recv()

        def first(self):
            self.start(0, 1, 2, 3, 4)

        def relay(self):
            self.wait(2 * c_y + core)
            self.start(5, 6, 10)
            self.wait(2 * c_2 + core)
            self.start(7, 11)
            self.wait(2 * c_p + core)
            self.start(8)
            self.wait(2 * c_m + core)
            self.start(9)

        def late(self):
            for i, c in ((12, c_yp), (13, c_ym), (14, c_y2)):
                self.wait(2 * c + core)
                self.start(i)

        def from_sib(self, c):
            self.wait(2 * c + (1 - core))

        def drain(self):
            ops = self.ops()
            for i in range(15):
                self.copy(i, *ops[i]).wait_send()

    def x_copy(c):
        return pltpu.make_async_copy(
            x_hbm.at[:, pl.ds(pl.multiple_of(c * 2 * KB, 2 * KB), 2 * KB)], xv.at[c], x_sem.at[c]
        )

    w_c = pltpu.make_async_copy(w_hbm, wraw, in_sem.at[0])
    kv_c = pltpu.make_async_copy(kv_hbm, kv, in_sem.at[1])
    dq_c = pltpu.make_async_copy(dq_hbm, dq, in_sem.at[2])
    dkv_c = pltpu.make_async_copy(dkv_hbm, dkv, in_sem.at[3])
    wout_c = pltpu.make_async_copy(wout_hbm, wout, in_sem.at[4])
    w_c.start()
    dq_c.start()
    dkv_c.start()
    kv_c.start()

    barrier = pltpu.get_barrier_semaphore()

    def greet_role(d, _):
        pl.semaphore_signal(barrier, inc=1, device_id=((me + d) % NR, tp), device_id_type=MESH)
        return 0

    lax.fori_loop(1, NR, greet_role, 0)
    for d in range(1, 4):
        pl.semaphore_signal(barrier, inc=1, device_id=(me, 4 * yl + (xx + d) % 4), device_id_type=MESH)
    pl.semaphore_signal(barrier, inc=1, device_id=(me, 4 * (1 - yl) + xx), device_id_type=MESH)

    chips = (chip, c_p, c_m, c_y, c_2, c_yp, c_ym, c_y2)
    for c in chips:
        x_copy(c).start()
    wout_c.start()

    lane = lax.broadcasted_iota(jnp.int32, (8, 128), 1)
    owners = [owner_ref[i, 0] for i in range(NP)]
    tags = jnp.full((8, 128), -1, jnp.int32)
    slots = []
    for i in range(NP):
        rank = jnp.int32(0)
        for j in range(i):
            rank = rank + (owners[j] == owners[i]).astype(jnp.int32)
        slot = 2 * owners[i] + rank
        slots.append(slot)
        slot_of[i] = slot
        tags = jnp.where(lane == slot, req_ref[i], tags)
    vtag[...] = tags
    rtag[me] = tags

    w_c.wait()
    eye = lax.broadcasted_iota(jnp.int32, (128, 128), 0) == lax.broadcasted_iota(jnp.int32, (128, 128), 1)
    for i in range(KB // 128):
        g = jnp.broadcast_to(gain_ref[me, i : i + 1, :], (128, 128))
        g = jnp.sum(jnp.where(eye, g, 0.0), axis=1, keepdims=True)
        rows = slice(128 * i, 128 * i + 128)
        wv[me, rows, :] = (wraw[rows, :].astype(F32) * g).astype(BF)

    dq_c.wait()
    for s in range(STEPS):
        for h in range(PER):
            qf[pl.ds(s * PER + h, RQ, stride=RQ), :] = dq[s, :, h * HS : (h + 1) * HS].astype(F32)

    def by_request(r, _):
        qb[r] = qf[pl.ds(pl.multiple_of(r * RQ, RQ), RQ), :].astype(BF)
        return 0

    lax.fori_loop(0, RQ, by_request, 0, unroll=4)

    pl.semaphore_wait(barrier, NR - 1 + 4)

    def send_tag(d, _):
        p = (me + d) % NR
        rc(vtag, rtag.at[me], tag_ss.at[d], tag_rs.at[me], p).start()
        return 0

    lax.fori_loop(1, NR, send_tag, 0)
    w_all = Gather(lambda r: wv.at[r], lambda i: w_ss.at[i], lambda r: w_rs.at[r])
    w_all.first()

    def find_page(s, _):
        i = jnp.int32(0)
        for j in range(NP):
            i = jnp.where(slots[j] == s, j, i)
        page_of[s] = i
        return 0

    lax.fori_loop(0, 2 * NR, find_page, 0)

    acc[...] = jnp.zeros_like(acc)
    sq[...] = jnp.zeros_like(sq)

    dkv_c.wait()
    kv_c.wait()

    def attend(r, _):
        q = qb[r]
        pages = [kv[bt_ref[r, j]] for j in range(4)]
        own = dkv[...]
        keys = jnp.concatenate([p[:, :HS] for p in pages], axis=0)
        values = jnp.concatenate([p[:, HS:] for p in pages], axis=0)
        s1 = lax.dot_general(q, keys, NT_DIMS, preferred_element_type=F32) * SCALING
        s2 = lax.dot_general(q, own[:, :HS], NT_DIMS, preferred_element_type=F32) * SCALING
        col = lax.broadcasted_iota(jnp.int32, s1.shape, 1)
        s1 = jnp.where(col < len_ref[r], s1, LOW)
        col2 = lax.broadcasted_iota(jnp.int32, s2.shape, 1)
        row2 = lax.broadcasted_iota(jnp.int32, s2.shape, 0)
        s2 = jnp.where((col2 % RQ == r) & (col2 // RQ <= row2 // PER), s2, LOW)
        top = jnp.maximum(jnp.max(s1, axis=1, keepdims=True), jnp.max(s2, axis=1, keepdims=True))
        p1 = jnp.exp(s1 - top)
        p2 = jnp.exp(s2 - top)
        total = jnp.sum(p1, axis=1, keepdims=True) + jnp.sum(p2, axis=1, keepdims=True)
        o = jnp.dot(p1.astype(BF), values, preferred_element_type=F32)
        o = o + jnp.dot(p2.astype(BF), own[:, HS:], preferred_element_type=F32)
        ac[pl.ds(r, RQ, stride=RQ), :] = o / total
        lc[pl.ds(r, RQ, stride=RQ), :] = jnp.broadcast_to(top + jnp.log(total), (RQ, HS))
        return 0

    lax.fori_loop(0, RQ // 2, attend, 0, unroll=UNROLL)

    tmat = jnp.full((8, 128), -1, jnp.int32)

    def wait_tag(d, t):
        p = (me - d + NR) % NR

        @pl.when(d > 0)
        def _():
            rc(vtag, rtag.at[p], tag_ss.at[0], tag_rs.at[p], p).wait_recv()

        moved = pltpu.roll(rtag[p], (2 * p - 2 * me + 128) % 128, 1)
        return jnp.where(lane // 2 == p, moved, t)

    tmat = lax.fori_loop(0, NR, wait_tag, tmat)
    tvec[...] = tmat
    t_c = pltpu.make_async_copy(tvec, tsm, t_sem)
    t_c.start()
    t_c.wait()

    def pick(s, _):
        qs[s] = qb[jnp.maximum(tsm[0, s], 0)]
        return 0

    lax.fori_loop(0, 2 * NR, pick, 0, unroll=4)

    def send_q(d, _):
        p = (me + d) % NR
        rc(qs.at[pl.ds(2 * p, 2)], qr.at[pl.ds(2 * me, 2)], q_ss.at[d], q_rs.at[me], p).start()
        return 0

    lax.fori_loop(1, NR, send_q, 0)
    qr[pl.ds(2 * me, 2)] = qs[pl.ds(2 * me, 2)]

    w_all.relay()
    lax.fori_loop(RQ // 2, RQ, attend, 0, unroll=UNROLL)

    def project(c):
        x_copy(c).wait()

        def tile(t, _):
            rows = pl.ds(pl.multiple_of(t * TILE, TILE), TILE)
            xa = xv[c, rows, :]
            acc[rows, :] += jnp.dot(xa, wv[pl.ds(2 * c, 2)].reshape(2 * KB, KVW), preferred_element_type=F32)
            part = sq[rows, :]
            for i in range(2 * KB // 128):
                xf = xa[:, i * 128 : i * 128 + 128].astype(F32)
                part = part + xf * xf
            sq[rows, :] = part
            return 0

        lax.fori_loop(0, ROWS // TILE, tile, 0)

    w_all.wait(sib)
    project(chip)
    for c in (c_p, c_m, c_y, c_2):
        w_all.from_sib(c)
        project(c)
    w_all.late()
    for c in (c_yp, c_ym, c_y2):
        w_all.from_sib(c)
        project(c)

    def wait_q(d, _):
        p = (me - d + NR) % NR
        rc(qs.at[pl.ds(0, 2)], qr.at[pl.ds(2 * p, 2)], q_ss.at[0], q_rs.at[p], p).wait_recv()
        return 0

    lax.fori_loop(1, NR, wait_q, 0)
    bias = bias_ref[...].astype(F32)
    lane_k = lax.broadcasted_iota(jnp.int32, (RQ, 128), 1)

    def page(i, st):
        rows = pl.ds(pl.multiple_of(i * PAGE, PAGE), PAGE)
        inverse = lax.rsqrt(jnp.sum(sq[rows, :], axis=1, keepdims=True) * (1.0 / (NR * KB)) + EPSILON)
        f = (acc[rows, :] * inverse + bias).astype(BF)
        slot = slot_of[i]
        q = qr[slot]
        s = lax.dot_general(q, f[:, :HS], NT_DIMS, preferred_element_type=F32) * SCALING
        top = jnp.max(s, axis=1, keepdims=True)
        p = jnp.exp(s - top)
        total = jnp.sum(p, axis=1, keepdims=True)
        o = jnp.dot(p.astype(BF), f[:, HS:], preferred_element_type=F32) / total
        pacc[i] = o.astype(BF)
        return jnp.where(lane_k == slot, top + jnp.log(total), st)

    st = lax.fori_loop(0, NP, page, jnp.full((RQ, 128), LOW, F32), unroll=True)
    packed = st[0:8]
    for a in range(1, 4):
        packed = jnp.where(lane // 32 == a, pltpu.roll(st[8 * a : 8 * a + 8], 32 * a, 1), packed)
    sst[...] = packed
    rst[me] = packed

    def place(s, _):
        accs[s] = pacc[page_of[s]]
        return 0

    lax.fori_loop(0, 2 * NR, place, 0, unroll=4)

    def send_acc(d, _):
        p = (me + d) % NR
        rc(accs.at[pl.ds(2 * p, 2)], racc.at[pl.ds(2 * me, 2)], a_ss.at[d], a_rs.at[me], p).start()
        rc(sst, rst.at[me], l_ss.at[d], l_rs.at[me], p).start()
        return 0

    lax.fori_loop(1, NR, send_acc, 0)
    racc[pl.ds(2 * me, 2)] = accs[pl.ds(2 * me, 2)]

    lt[...] = jnp.full((RQ, 128), LOW, F32)

    def wait_acc(d, _):
        p = (me - d + NR) % NR
        rc(sst, rst.at[p], l_ss.at[0], l_rs.at[p], p).wait_recv()
        rc(accs.at[pl.ds(0, 2)], racc.at[pl.ds(2 * p, 2)], a_ss.at[0], a_rs.at[p], p).wait_recv()
        return 0

    lax.fori_loop(1, NR, wait_acc, 0)

    def take(p, _):
        got = rst[p]
        for a in range(4):
            moved = pltpu.roll(got, (2 * p - 2 * me - 32 * a + 256) % 128, 1)
            lt[8 * a : 8 * a + 8, :] = jnp.where(lane // 2 == p, moved, lt[8 * a : 8 * a + 8, :])
        for c in range(2):
            sb[pl.ds(2 * p + c, RQ, stride=RQ), :] = racc[2 * p + c].astype(F32)
        return 0

    lax.fori_loop(0, NR, take, 0, unroll=4)

    mine = jnp.broadcast_to(tvec[0:1, :], (RQ, 128)) == lax.broadcasted_iota(jnp.int32, (RQ, 128), 0)

    def outputs(s):
        return Gather(lambda r: aall.at[s, r], lambda i: g_ss.at[s, i], lambda r: g_rs.at[s, r])

    def merge(s):
        for h in range(PER):
            k = s * PER + h
            rows = pl.ds(pl.multiple_of(k * RQ, RQ), RQ)
            scores = jnp.where(mine, jnp.broadcast_to(lt[pl.ds(k, 1), :], (RQ, 128)), LOW)
            base = lc[rows, :]
            top = jnp.maximum(jnp.max(scores, axis=1, keepdims=True), base)
            e = jnp.exp(scores - top)
            wc = jnp.exp(base - top)
            total = wc + jnp.sum(e, axis=1, keepdims=True)
            pv = jnp.dot(e[:, : 2 * NR].astype(BF), sb[rows, :].astype(BF), preferred_element_type=F32)
            merged = (wc * ac[rows, :] + pv) / total
            aall[s, me, :, h * HS : (h + 1) * HS] = merged.astype(BF)
        outputs(s).first()

    def x_send(s, d):
        to = (xx + d) % 4
        return rc(ps.at[s, to], px.at[s, xx], p_ss.at[s, d], p_rs.at[s, xx], me, 4 * yl + to)

    def x_wait(s, d):
        of = (xx + d) % 4
        rc(ps.at[s, 0], px.at[s, of], p_ss.at[s, 0], p_rs.at[s, of], me, 4 * yl + of).wait_recv()

    def y_send(s):
        return rc(ys.at[s], py.at[s], y_ss.at[s], y_rs.at[s], me, 4 * (1 - yl) + xx)

    def product(s):
        g = outputs(s)
        g.late()
        g.wait(sib)
        for c in chips[1:]:
            g.from_sib(c)

        def part(j, _):
            a = aall[s, pl.ds(j * 8, 8)].reshape(8 * RQ, 1024)
            o = jnp.dot(a, wout[...], preferred_element_type=F32).astype(BF)
            o = o.reshape(4, 2 * RQ, NOUT)
            for i in range(4):
                ps[s, i, j] = o[i]
            return 0

        lax.fori_loop(0, 2, part, 0)
        for d in range(1, 4):
            x_send(s, d).start()

    def add_x(s):
        for d in range(1, 4):
            x_wait(s, d)
        for half in range(2):
            o = ps[s, xx, half].astype(F32)
            for d in range(1, 4):
                o = o + px[s, (xx + d) % 4, half].astype(F32)

            @pl.when(yl == half)
            def _():
                ko[s] = o

            @pl.when(yl != half)
            def _():
                ys[s] = o.astype(BF)

        y_send(s).start()

    def add_y(s):
        y_send(s).wait_recv()
        out_ref[s] = (ko[s] + py[s].astype(F32)).astype(BF)

    merge(0)
    merge(1)
    wout_c.wait()

    def round_(i, _):
        @pl.when(i < STEPS)
        def _():
            outputs(i).relay()

        @pl.when(i < STEPS - 2)
        def _():
            merge(i + 2)

        @pl.when((i >= 1) & (i <= STEPS))
        def _():
            product(i - 1)

        @pl.when((i >= 2) & (i <= STEPS + 1))
        def _():
            add_x(i - 2)

        @pl.when(i >= 3)
        def _():
            add_y(i - 3)

        return 0

    lax.fori_loop(0, STEPS + 3, round_, 0)

    def drain(d, _):
        rc(vtag, rtag.at[me], tag_ss.at[d], tag_rs.at[me], sib).wait_send()
        rc(qs.at[pl.ds(0, 2)], qr.at[pl.ds(0, 2)], q_ss.at[d], q_rs.at[me], sib).wait_send()
        rc(accs.at[pl.ds(0, 2)], racc.at[pl.ds(0, 2)], a_ss.at[d], a_rs.at[me], sib).wait_send()
        rc(sst, rst.at[me], l_ss.at[d], l_rs.at[me], sib).wait_send()
        return 0

    lax.fori_loop(1, NR, drain, 0)
    w_all.drain()

    def drain_s(s, _):
        outputs(s).drain()
        for d in range(1, 4):
            x_send(s, d).wait_send()
        y_send(s).wait_send()
        return 0

    lax.fori_loop(0, STEPS, drain_s, 0)


def body(
    x_pre,
    ln_gain,
    w_kv,
    kv_bias,
    page_owner,
    page_req,
    kv_pool,
    block_table,
    cache_len,
    dec_q,
    dec_kv,
    w_out,
):
    any_spec = pl.BlockSpec(memory_space=pl.ANY)
    smem = pl.BlockSpec(memory_space=pltpu.SMEM)
    vmem = pl.BlockSpec(memory_space=pltpu.VMEM)
    dma = pltpu.SemaphoreType.DMA
    V = pltpu.VMEM
    scratch = [
        V((8, ROWS, 2 * KB), BF),
        V((KB, KVW), BF),
        V((NR, KB, KVW), BF),
        V((32, PAGE, KVW), BF),
        V((STEPS, RQ, 1024), BF),
        V((STEPS * RQ, KVW), BF),
        V((1024, NOUT), BF),
        V((ROWS, KVW), F32),
        V((ROWS, 128), F32),
        V((RQ * RQ, HS), F32),
        V((RQ, RQ, HS), BF),
        V((RQ * RQ, HS), F32),
        V((RQ * RQ, HS), F32),
        V((8, 128), jnp.int32),
        V((NR, 8, 128), jnp.int32),
        V((8, 128), jnp.int32),
        pltpu.SMEM((8, 128), jnp.int32),
        pltpu.SMEM((16,), jnp.int32),
        pltpu.SMEM((2 * NR,), jnp.int32),
        V((2 * NR, RQ, HS), BF),
        V((2 * NR, RQ, HS), BF),
        V((NP, RQ, HS), BF),
        V((2 * NR, RQ, HS), BF),
        V((2 * NR, RQ, HS), BF),
        V((8, 128), F32),
        V((NR, 8, 128), F32),
        V((RQ, 128), F32),
        V((RQ * RQ, HS), F32),
        V((STEPS, NR, RQ, 1024), BF),
        V((STEPS, 4, 2, 2 * RQ, NOUT), BF),
        V((STEPS, 4, 2, 2 * RQ, NOUT), BF),
        V((STEPS, 2 * RQ, NOUT), BF),
        V((STEPS, 2 * RQ, NOUT), BF),
        V((STEPS, 2 * RQ, NOUT), F32),
        dma((8,)),
        dma((5,)),
        dma,
        dma((15,)),
        dma((NR,)),
        dma((NR,)),
        dma((NR,)),
        dma((NR,)),
        dma((NR,)),
        dma((NR,)),
        dma((NR,)),
        dma((NR,)),
        dma((NR,)),
        dma((STEPS, 15)),
        dma((STEPS, NR)),
        dma((STEPS, 4)),
        dma((STEPS, 4)),
        dma((STEPS,)),
        dma((STEPS,)),
    ]
    return pl.pallas_call(
        kernel,
        out_shape=jax.ShapeDtypeStruct((STEPS, 2 * RQ, NOUT), BF),
        in_specs=[any_spec, vmem, any_spec, vmem, smem, smem, any_spec, smem, smem, any_spec, any_spec, any_spec],
        out_specs=vmem,
        scratch_shapes=scratch,
        compiler_params=pltpu.CompilerParams(
            collective_id=0, has_side_effects=True, vmem_limit_bytes=58 * 1024 * 1024
        ),
    )(
        x_pre,
        ln_gain.reshape(NR, KB // 128, 128).astype(F32),
        w_kv,
        kv_bias.reshape(1, KVW),
        page_owner,
        page_req,
        kv_pool,
        block_table,
        cache_len,
        dec_q,
        dec_kv.reshape(STEPS * RQ, KVW),
        w_out,
    )


def solution(mesh):
    return jax.shard_map(
        body,
        mesh=mesh,
        in_specs=(
            P("role", None),
            P(),
            P("role", "tp"),
            P("tp"),
            P("role", None),
            P("role"),
            P("role", None, "tp"),
            P("role", None),
            P("role"),
            P(None, "role", "tp"),
            P(None, "role", "tp"),
            P("tp", "role"),
        ),
        out_specs=P(None, "tp", "role"),
        check_vma=False,
    )
```

time: 117 us -> 107 us (0.915)
  Pallas kernels: 110 us -> 99.9 us
  local copies, waits for them, and re-layouts: 4.3 us -> 5.59 us
  other arithmetic: 2.54 us -> 1.34 us
    pallas_call x1, Pallas kernels: 110 us -> 99.9 us  [body(): pl.pallas_call(kernel, out_shape=jax.ShapeDtypeStruct((STEPS, 2 * RQ, NOU...]
    unnamed x2 -> x3, local copies, waits for them, and re-layouts: 2.43 us -> 4.36 us
    convert_element_type x2 -> x1, other arithmetic: 2.54 us -> 1.34 us  [body(): ln_gain.reshape(NR, KB // 128, 128).astype(F32)]
where the time goes in v2:
time: 107 us
  Pallas kernels  99.9 us (93%)
  local copies, waits for them, and re-layouts  5.59 us (5%)
  other arithmetic  1.34 us (1%)
    pallas_call x1, Pallas kernels, body(): pl.pallas_call(kernel, out_shape=jax.ShapeDtypeStruct((STEPS, 2 * RQ, NOU...  99.9 us
    unnamed x3, local copies, waits for them, and re-layouts  4.36 us

profile of v2, /device:TPU:1, one launch (start us, length us, event | category | flops | bytes accessed | tf_op | source)
XLA Modules:
  0.0 106.8 jit_solution(11194269731017544310)
XLA Ops:
  0.0 1.2 %reshape.9.bias_ref = bf16[1,256]{1,0:T(2,128)(2,1)} reshape(bf16[256]{0:T(256)(128)(2,1)} %param.15) | data formatting | bytes 1024 | tf_op jit(solution)/shard_map/reshape | solution.py:631
  1.2 1.3 %copy.13.owner_ref = s32[11,1]{1,0:T(8,128)} copy(s32[11,1]{0,1:T(1,128)} %param.16) | data formatting | bytes 88 | tf_op args[4]
  2.6 1.4 %copy.14.bt_ref = s32[32,4]{1,0:T(8,128)} copy(s32[32,4]{0,1:T(4,128)} %param.19) | data formatting | bytes 1024 | tf_op args[7]
  3.9 1.3 %convert.1.gain_ref = f32[16,4,128]{2,1,0:T(4,128)} convert(bf16[16,4,128]{2,1,0:T(4,128)(2,1)} %bitcast.4) | non-fusion elementwise | flops 8192 | bytes 49152 | tf_op jit(solution)/shard_map/convert_element_type | solution.py:629
  5.3 99.9 %shard_map.118 = bf16[4,64,512]{2,1,0:T(8,128)(2,1)} custom-call(bf16[1408,8192]{1,0:T(8,128)(2,1)} %x_hbm.1, f32[16,4,128]{2,1,0:T(4,128)} %convert.1.gain_ref, bf16[512,256]{1,0:T(8,128)(2,1)} %w_hbm.1, bf16[1,256]{1,0:T(2,128)(2,1)} %reshape.9.bias_ref, s32[11,1]{1,0:T(8,128)} %copy.13.owner_ref, s32[11]{0:T(128)} %req_ref.1, ...), custom_call_target="tpu_custom_call" | custom-call | tf_op jit(solution)/shard_map/pallas_call | solution.py:618
  105.1 1.7 %copy.16 = bf16[4,64,512]{2,1,0:T(8,128)(2,1)} copy(bf16[4,64,512]{2,1,0:T(8,128)(2,1)} %shard_map.118) | data formatting | bytes 524288

commit v3 on v2

--- a/solution.py
+++ b/solution.py
@@ -25,8 +25,8 @@
 KB = 512
 KVW = 256
 ROWS = NP * PAGE
-TILE = 352
-UNROLL = 2
+TILE = 704
+UNROLL = 4
 NOUT = 512
 SCALING = 1.0 / math.sqrt(HS)
 NT_DIMS = (((1,), (1,)), ((), ()))
@@ -209,7 +209,7 @@
     wout_c.start()
 
     lane = lax.broadcasted_iota(jnp.int32, (8, 128), 1)
-    owners = [owner_ref[i, 0] for i in range(NP)]
+    owners = [owner_ref[0, i] for i in range(NP)]
     tags = jnp.full((8, 128), -1, jnp.int32)
     slots = []
     for i in range(NP):
@@ -225,8 +225,9 @@
 
     w_c.wait()
     eye = lax.broadcasted_iota(jnp.int32, (128, 128), 0) == lax.broadcasted_iota(jnp.int32, (128, 128), 1)
+    gain = gain_ref[me].astype(F32)
     for i in range(KB // 128):
-        g = jnp.broadcast_to(gain_ref[me, i : i + 1, :], (128, 128))
+        g = jnp.broadcast_to(gain[i : i + 1, :], (128, 128))
         g = jnp.sum(jnp.where(eye, g, 0.0), axis=1, keepdims=True)
         rows = slice(128 * i, 128 * i + 128)
         wv[me, rows, :] = (wraw[rows, :].astype(F32) * g).astype(BF)
@@ -270,7 +271,7 @@
 
     def attend(r, _):
         q = qb[r]
-        pages = [kv[bt_ref[r, j]] for j in range(4)]
+        pages = [kv[bt_ref[j, r]] for j in range(4)]
         own = dkv[...]
         keys = jnp.concatenate([p[:, :HS] for p in pages], axis=0)
         values = jnp.concatenate([p[:, HS:] for p in pages], axis=0)
@@ -361,6 +362,7 @@
 
     lax.fori_loop(1, NR, wait_q, 0)
     bias = bias_ref[...].astype(F32)
+    bias = jnp.concatenate([bias[0:1], bias[1:2]], axis=1)
     lane_k = lax.broadcasted_iota(jnp.int32, (RQ, 128), 1)
 
     def page(i, st):
@@ -626,13 +628,13 @@
         ),
     )(
         x_pre,
-        ln_gain.reshape(NR, KB // 128, 128).astype(F32),
+        ln_gain.reshape(NR, KB // 128, 128),
         w_kv,
-        kv_bias.reshape(1, KVW),
-        page_owner,
+        kv_bias.reshape(2, HS),
+        page_owner.T,
         page_req,
         kv_pool,
-        block_table,
+        block_table.T,
         cache_len,
         dec_q,
         dec_kv.reshape(STEPS * RQ, KVW),

time: 107 us -> 98 us (0.916)
  local copies, waits for them, and re-layouts: 5.59 us -> 1.67 us
  Pallas kernels: 99.9 us -> 96.1 us
  other arithmetic: 1.34 us -> 0 us
    pallas_call x1, Pallas kernels: 99.9 us -> 96.1 us  [body(): pl.pallas_call(kernel, out_shape=jax.ShapeDtypeStruct((STEPS, 2 * RQ, NOU...]
    unnamed x3 -> x1, local copies, waits for them, and re-layouts: 4.36 us -> 1.67 us
    convert_element_type x1 -> x0, other arithmetic: 1.34 us -> none  [body(): ln_gain.reshape(NR, KB // 128, 128).astype(F32)]
    reshape x1 -> x0, local copies, waits for them, and re-layouts: 1.23 us -> none  [body(): kv_bias.reshape(1, KVW)]
where the time goes in v3:
time: 98 us; the launch traced here: 97.8 us
  Pallas kernels  96.1 us (98%)
  local copies, waits for them, and re-layouts  1.67 us (2%)
    pallas_call x1, Pallas kernels, body(): pl.pallas_call(kernel, out_shape=jax.ShapeDtypeStruct((STEPS, 2 * RQ, NOU...  96.1 us

profile of v3, /device:TPU:1, one launch (start us, length us, event | category | flops | bytes accessed | tf_op | source)
XLA Modules:
  0.0 97.8 jit_solution(10997144447983994115)
XLA Ops:
  0.0 96.1 %shard_map.118 = bf16[4,64,512]{2,1,0:T(8,128)(2,1)} custom-call(bf16[1408,8192]{1,0:T(8,128)(2,1)} %x_hbm.1, bf16[16,4,128]{2,1,0:T(4,128)(2,1)} %bitcast.6, bf16[512,256]{1,0:T(8,128)(2,1)} %w_hbm.1, bf16[2,128]{1,0:T(2,128)(2,1)} %bitcast.8, s32[1,11]{1,0:T(1,128)} %bitcast.9, s32[11]{0:T(128)} %req_ref.1, bf16[32,128,256]{2,1,0:T(8,128)(2,1)} %kv_hbm.1, ...), custom_call_target="tpu_custom_call" | custom-call | tf_op jit(solution)/shard_map/pallas_call | solution.py:620
  96.1 1.7 %copy.14 = bf16[4,64,512]{2,1,0:T(8,128)(2,1)} copy(bf16[4,64,512]{2,1,0:T(8,128)(2,1)} %shard_map.118) | data formatting | bytes 524288

commit v4 on v3

--- a/solution.py
+++ b/solution.py
@@ -76,6 +76,7 @@
     sb,
     aall,
     ps,
+    pa,
     px,
     ys,
     py,
@@ -154,15 +155,17 @@
         def first(self):
             self.start(0, 1, 2, 3, 4)
 
-        def relay(self):
+        def relay_near(self):
             self.wait(2 * c_y + core)
             self.start(5, 6, 10)
-            self.wait(2 * c_2 + core)
-            self.start(7, 11)
             self.wait(2 * c_p + core)
             self.start(8)
             self.wait(2 * c_m + core)
             self.start(9)
+
+        def relay_far(self):
+            self.wait(2 * c_2 + core)
+            self.start(7, 11)
 
         def late(self):
             for i, c in ((12, c_yp), (13, c_ym), (14, c_y2)):
@@ -199,7 +202,7 @@
         return 0
 
     lax.fori_loop(1, NR, greet_role, 0)
-    for d in range(1, 4):
+    for d in (1, 3):
         pl.semaphore_signal(barrier, inc=1, device_id=(me, 4 * yl + (xx + d) % 4), device_id_type=MESH)
     pl.semaphore_signal(barrier, inc=1, device_id=(me, 4 * (1 - yl) + xx), device_id_type=MESH)
 
@@ -243,7 +246,7 @@
 
     lax.fori_loop(0, RQ, by_request, 0, unroll=4)
 
-    pl.semaphore_wait(barrier, NR - 1 + 4)
+    pl.semaphore_wait(barrier, NR - 1 + 3)
 
     def send_tag(d, _):
         p = (me + d) % NR
@@ -292,42 +295,38 @@
         lc[pl.ds(r, RQ, stride=RQ), :] = jnp.broadcast_to(top + jnp.log(total), (RQ, HS))
         return 0
 
-    lax.fori_loop(0, RQ // 2, attend, 0, unroll=UNROLL)
-
-    tmat = jnp.full((8, 128), -1, jnp.int32)
-
-    def wait_tag(d, t):
-        p = (me - d + NR) % NR
-
-        @pl.when(d > 0)
-        def _():
-            rc(vtag, rtag.at[p], tag_ss.at[0], tag_rs.at[p], p).wait_recv()
-
-        moved = pltpu.roll(rtag[p], (2 * p - 2 * me + 128) % 128, 1)
-        return jnp.where(lane // 2 == p, moved, t)
-
-    tmat = lax.fori_loop(0, NR, wait_tag, tmat)
-    tvec[...] = tmat
-    t_c = pltpu.make_async_copy(tvec, tsm, t_sem)
-    t_c.start()
-    t_c.wait()
-
-    def pick(s, _):
-        qs[s] = qb[jnp.maximum(tsm[0, s], 0)]
-        return 0
-
-    lax.fori_loop(0, 2 * NR, pick, 0, unroll=4)
-
-    def send_q(d, _):
-        p = (me + d) % NR
-        rc(qs.at[pl.ds(2 * p, 2)], qr.at[pl.ds(2 * me, 2)], q_ss.at[d], q_rs.at[me], p).start()
-        return 0
-
-    lax.fori_loop(1, NR, send_q, 0)
-    qr[pl.ds(2 * me, 2)] = qs[pl.ds(2 * me, 2)]
-
-    w_all.relay()
-    lax.fori_loop(RQ // 2, RQ, attend, 0, unroll=UNROLL)
+    def ask():
+        tmat = jnp.full((8, 128), -1, jnp.int32)
+
+        def wait_tag(d, t):
+            p = (me - d + NR) % NR
+
+            @pl.when(d > 0)
+            def _():
+                rc(vtag, rtag.at[p], tag_ss.at[0], tag_rs.at[p], p).wait_recv()
+
+            moved = pltpu.roll(rtag[p], (2 * p - 2 * me + 128) % 128, 1)
+            return jnp.where(lane // 2 == p, moved, t)
+
+        tmat = lax.fori_loop(0, NR, wait_tag, tmat)
+        tvec[...] = tmat
+        t_c = pltpu.make_async_copy(tvec, tsm, t_sem)
+        t_c.start()
+        t_c.wait()
+
+        def pick(s, _):
+            qs[s] = qb[jnp.maximum(tsm[0, s], 0)]
+            return 0
+
+        lax.fori_loop(0, 2 * NR, pick, 0, unroll=4)
+
+        def send_q(d, _):
+            p = (me + d) % NR
+            rc(qs.at[pl.ds(2 * p, 2)], qr.at[pl.ds(2 * me, 2)], q_ss.at[d], q_rs.at[me], p).start()
+            return 0
+
+        lax.fori_loop(1, NR, send_q, 0)
+        qr[pl.ds(2 * me, 2)] = qs[pl.ds(2 * me, 2)]
 
     def project(c):
         x_copy(c).wait()
@@ -345,15 +344,33 @@
 
         lax.fori_loop(0, ROWS // TILE, tile, 0)
 
-    w_all.wait(sib)
-    project(chip)
-    for c in (c_p, c_m, c_y, c_2):
+    def group(i, _):
+        lax.fori_loop(0, 8, lambda r, carry: attend(8 * i + r, carry), 0, unroll=UNROLL)
+
+        @pl.when(i == 1)
+        def _():
+            ask()
+            w_all.relay_near()
+
+        @pl.when(i == 2)
+        def _():
+            w_all.wait(sib)
+            project(chip)
+            w_all.relay_far()
+
+        return 0
+
+    lax.fori_loop(0, RQ // 8, group, 0)
+
+    def next_chip(i, _):
+        c = chip_at(i % 4, i // 4)
         w_all.from_sib(c)
         project(c)
+        return 0
+
+    lax.fori_loop(1, 5, next_chip, 0)
     w_all.late()
-    for c in (c_yp, c_ym, c_y2):
-        w_all.from_sib(c)
-        project(c)
+    lax.fori_loop(5, 8, next_chip, 0)
 
     def wait_q(d, _):
         p = (me - d + NR) % NR
@@ -442,13 +459,27 @@
             aall[s, me, :, h * HS : (h + 1) * HS] = merged.astype(BF)
         outputs(s).first()
 
-    def x_send(s, d):
-        to = (xx + d) % 4
-        return rc(ps.at[s, to], px.at[s, xx], p_ss.at[s, d], p_rs.at[s, xx], me, 4 * yl + to)
-
-    def x_wait(s, d):
-        of = (xx + d) % 4
-        rc(ps.at[s, 0], px.at[s, of], p_ss.at[s, 0], p_rs.at[s, of], me, 4 * yl + of).wait_recv()
+    x_p, x_m, x_2 = (xx + 1) % 4, (xx + 3) % 4, (xx + 2) % 4
+
+    def x_send(s, i):
+        to = x_m if i % 2 else x_p
+        src, dst = (
+            (ps.at[s, x_2, 0], pa.at[s, 0]),
+            (ps.at[s, x_2, 1], pa.at[s, 1]),
+            (ps.at[s, x_p, 1], px.at[s, 0, 1]),
+            (ps.at[s, x_m, 0], px.at[s, 1, 0]),
+            (ps.at[s, x_p, 0], px.at[s, 0, 0]),
+            (ps.at[s, x_m, 1], px.at[s, 1, 1]),
+        )[i]
+        return rc(src, dst, p_ss.at[s, i], p_rs.at[s, i], me, 4 * yl + to)
+
+    def relay_x(s):
+        x_send(s, 0).wait_recv()
+        ps[s, x_p, 0] = (ps[s, x_p, 0].astype(F32) + pa[s, 0].astype(F32)).astype(BF)
+        x_send(s, 4).start()
+        x_send(s, 1).wait_recv()
+        ps[s, x_m, 1] = (ps[s, x_m, 1].astype(F32) + pa[s, 1].astype(F32)).astype(BF)
+        x_send(s, 5).start()
 
     def y_send(s):
         return rc(ys.at[s], py.at[s], y_ss.at[s], y_rs.at[s], me, 4 * (1 - yl) + xx)
@@ -465,20 +496,25 @@
             o = jnp.dot(a, wout[...], preferred_element_type=F32).astype(BF)
             o = o.reshape(4, 2 * RQ, NOUT)
             for i in range(4):
-                ps[s, i, j] = o[i]
+                for h in range(2):
+                    ps[s, i, h, j] = o[i, :, h * 256 : h * 256 + 256]
             return 0
 
         lax.fori_loop(0, 2, part, 0)
-        for d in range(1, 4):
-            x_send(s, d).start()
+        for i in range(4):
+            x_send(s, i).start()
 
     def add_x(s):
-        for d in range(1, 4):
-            x_wait(s, d)
+        for i in range(2, 6):
+            x_send(s, i).wait_recv()
         for half in range(2):
-            o = ps[s, xx, half].astype(F32)
-            for d in range(1, 4):
-                o = o + px[s, (xx + d) % 4, half].astype(F32)
+            o = jnp.concatenate(
+                [
+                    ps[s, xx, h, half].astype(F32) + px[s, 0, h, half].astype(F32) + px[s, 1, h, half].astype(F32)
+                    for h in range(2)
+                ],
+                axis=1,
+            )
 
             @pl.when(yl == half)
             def _():
@@ -501,7 +537,8 @@
     def round_(i, _):
         @pl.when(i < STEPS)
         def _():
-            outputs(i).relay()
+            outputs(i).relay_near()
+            outputs(i).relay_far()
 
         @pl.when(i < STEPS - 2)
         def _():
@@ -513,15 +550,19 @@
 
         @pl.when((i >= 2) & (i <= STEPS + 1))
         def _():
-            add_x(i - 2)
-
-        @pl.when(i >= 3)
+            relay_x(i - 2)
+
+        @pl.when((i >= 3) & (i <= STEPS + 2))
         def _():
-            add_y(i - 3)
-
-        return 0
-
-    lax.fori_loop(0, STEPS + 3, round_, 0)
+            add_x(i - 3)
+
+        @pl.when(i >= 4)
+        def _():
+            add_y(i - 4)
+
+        return 0
+
+    lax.fori_loop(0, STEPS + 4, round_, 0)
 
     def drain(d, _):
         rc(vtag, rtag.at[me], tag_ss.at[d], tag_rs.at[me], sib).wait_send()
@@ -535,8 +576,8 @@
 
     def drain_s(s, _):
         outputs(s).drain()
-        for d in range(1, 4):
-            x_send(s, d).wait_send()
+        for i in range(6):
+            x_send(s, i).wait_send()
         y_send(s).wait_send()
         return 0
 
@@ -592,8 +633,9 @@
         V((RQ, 128), F32),
         V((RQ * RQ, HS), F32),
         V((STEPS, NR, RQ, 1024), BF),
-        V((STEPS, 4, 2, 2 * RQ, NOUT), BF),
-        V((STEPS, 4, 2, 2 * RQ, NOUT), BF),
+        V((STEPS, 4, 2, 2, 2 * RQ, 256), BF),
+        V((STEPS, 2, 2, 2 * RQ, 256), BF),
+        V((STEPS, 2, 2, 2, 2 * RQ, 256), BF),
         V((STEPS, 2 * RQ, NOUT), BF),
         V((STEPS, 2 * RQ, NOUT), BF),
         V((STEPS, 2 * RQ, NOUT), F32),
@@ -612,8 +654,8 @@
         dma((NR,)),
         dma((STEPS, 15)),
         dma((STEPS, NR)),
-        dma((STEPS, 4)),
-        dma((STEPS, 4)),
+        dma((STEPS, 6)),
+        dma((STEPS, 6)),
         dma((STEPS,)),
         dma((STEPS,)),
     ]

time: 98 us -> 89.6 us (0.914)
  Pallas kernels: 96.1 us -> 87.7 us
    pallas_call x1, Pallas kernels: 96.1 us -> 87.7 us  [body(): pl.pallas_call(kernel, out_shape=jax.ShapeDtypeStruct((STEPS, 2 * RQ, NOU...]
where the time goes in v4:
time: 89.6 us; the launch traced here: 89.4 us
  Pallas kernels  87.7 us (98%)
  local copies, waits for them, and re-layouts  1.67 us (2%)
    pallas_call x1, Pallas kernels, body(): pl.pallas_call(kernel, out_shape=jax.ShapeDtypeStruct((STEPS, 2 * RQ, NOU...  87.7 us

profile of v4, /device:TPU:1, one launch (start us, length us, event | category | flops | bytes accessed | tf_op | source)
XLA Modules:
  0.0 89.4 jit_solution(9527293198881041024)
XLA Ops:
  0.0 87.7 %shard_map.118 = bf16[4,64,512]{2,1,0:T(8,128)(2,1)} custom-call(bf16[1408,8192]{1,0:T(8,128)(2,1)} %x_hbm.1, bf16[16,4,128]{2,1,0:T(4,128)(2,1)} %bitcast.6, bf16[512,256]{1,0:T(8,128)(2,1)} %w_hbm.1, bf16[2,128]{1,0:T(2,128)(2,1)} %bitcast.8, s32[1,11]{1,0:T(1,128)} %bitcast.9, s32[11]{0:T(128)} %req_ref.1, bf16[32,128,256]{2,1,0:T(8,128)(2,1)} %kv_hbm.1, ...), custom_call_target="tpu_custom_call" | custom-call | tf_op jit(solution)/shard_map/pallas_call | solution.py:662
  87.8 1.7 %copy.14 = bf16[4,64,512]{2,1,0:T(8,128)(2,1)} copy(bf16[4,64,512]{2,1,0:T(8,128)(2,1)} %shard_map.118) | data formatting | bytes 524288

commit v5 on v4

--- a/solution.py
+++ b/solution.py
@@ -26,6 +26,7 @@
 KVW = 256
 ROWS = NP * PAGE
 TILE = 704
+SQ_TILE = 176
 UNROLL = 4
 NOUT = 512
 SCALING = 1.0 / math.sqrt(HS)
@@ -47,7 +48,6 @@
     wout_hbm,
     out_ref,
     xv,
-    wraw,
     wv,
     kv,
     dq,
@@ -185,7 +185,7 @@
             x_hbm.at[:, pl.ds(pl.multiple_of(c * 2 * KB, 2 * KB), 2 * KB)], xv.at[c], x_sem.at[c]
         )
 
-    w_c = pltpu.make_async_copy(w_hbm, wraw, in_sem.at[0])
+    w_c = pltpu.make_async_copy(w_hbm, wv.at[me], in_sem.at[0])
     kv_c = pltpu.make_async_copy(kv_hbm, kv, in_sem.at[1])
     dq_c = pltpu.make_async_copy(dq_hbm, dq, in_sem.at[2])
     dkv_c = pltpu.make_async_copy(dkv_hbm, dkv, in_sem.at[3])
@@ -206,7 +206,7 @@
         pl.semaphore_signal(barrier, inc=1, device_id=(me, 4 * yl + (xx + d) % 4), device_id_type=MESH)
     pl.semaphore_signal(barrier, inc=1, device_id=(me, 4 * (1 - yl) + xx), device_id_type=MESH)
 
-    chips = (chip, c_p, c_m, c_y, c_2, c_yp, c_ym, c_y2)
+    chips = [chip_at(i % 4, i // 4) for i in range(8)]
     for c in chips:
         x_copy(c).start()
     wout_c.start()
@@ -226,15 +226,6 @@
     vtag[...] = tags
     rtag[me] = tags
 
-    w_c.wait()
-    eye = lax.broadcasted_iota(jnp.int32, (128, 128), 0) == lax.broadcasted_iota(jnp.int32, (128, 128), 1)
-    gain = gain_ref[me].astype(F32)
-    for i in range(KB // 128):
-        g = jnp.broadcast_to(gain[i : i + 1, :], (128, 128))
-        g = jnp.sum(jnp.where(eye, g, 0.0), axis=1, keepdims=True)
-        rows = slice(128 * i, 128 * i + 128)
-        wv[me, rows, :] = (wraw[rows, :].astype(F32) * g).astype(BF)
-
     dq_c.wait()
     for s in range(STEPS):
         for h in range(PER):
@@ -245,6 +236,27 @@
         return 0
 
     lax.fori_loop(0, RQ, by_request, 0, unroll=4)
+
+    sq[...] = jnp.zeros_like(sq)
+
+    def squares(i, _):
+        c = chip_at(i % 4, i // 4)
+        x_copy(c).wait()
+
+        def tile(t, _):
+            rows = pl.ds(pl.multiple_of(t * SQ_TILE, SQ_TILE), SQ_TILE)
+            part = sq[rows, :]
+            for j in range(2 * KB // 128):
+                xf = xv[c, rows, j * 128 : j * 128 + 128].astype(F32)
+                part = part + xf * xf
+            sq[rows, :] = part
+            return 0
+
+        lax.fori_loop(0, ROWS // SQ_TILE, tile, 0)
+        return 0
+
+    lax.fori_loop(0, 4, squares, 0)
+    w_c.wait()
 
     pl.semaphore_wait(barrier, NR - 1 + 3)
 
@@ -267,7 +279,15 @@
     lax.fori_loop(0, 2 * NR, find_page, 0)
 
     acc[...] = jnp.zeros_like(acc)
-    sq[...] = jnp.zeros_like(sq)
+    lax.fori_loop(4, 8, squares, 0)
+
+    def invert(t, _):
+        rows = pl.ds(pl.multiple_of(t * PAGE, PAGE), PAGE)
+        mean = jnp.sum(sq[rows, :], axis=1, keepdims=True) * (1.0 / (NR * KB))
+        sq[rows, :] = jnp.broadcast_to(lax.rsqrt(mean + EPSILON), (PAGE, 128))
+        return 0
+
+    lax.fori_loop(0, NP, invert, 0)
 
     dkv_c.wait()
     kv_c.wait()
@@ -329,17 +349,16 @@
         qr[pl.ds(2 * me, 2)] = qs[pl.ds(2 * me, 2)]
 
     def project(c):
-        x_copy(c).wait()
-
         def tile(t, _):
             rows = pl.ds(pl.multiple_of(t * TILE, TILE), TILE)
-            xa = xv[c, rows, :]
-            acc[rows, :] += jnp.dot(xa, wv[pl.ds(2 * c, 2)].reshape(2 * KB, KVW), preferred_element_type=F32)
-            part = sq[rows, :]
-            for i in range(2 * KB // 128):
-                xf = xa[:, i * 128 : i * 128 + 128].astype(F32)
-                part = part + xf * xf
-            sq[rows, :] = part
+            inverse = sq[rows, :]
+            normed = []
+            for j in range(2 * KB // 128):
+                gain = gain_ref[2 * c + j // 4, j % 4 : j % 4 + 1, :].astype(F32)
+                xf = xv[c, rows, j * 128 : j * 128 + 128].astype(F32)
+                normed.append((xf * inverse * gain).astype(BF))
+            normed = jnp.concatenate(normed, axis=1)
+            acc[rows, :] += jnp.dot(normed, wv[pl.ds(2 * c, 2)].reshape(2 * KB, KVW), preferred_element_type=F32)
             return 0
 
         lax.fori_loop(0, ROWS // TILE, tile, 0)
@@ -384,8 +403,7 @@
 
     def page(i, st):
         rows = pl.ds(pl.multiple_of(i * PAGE, PAGE), PAGE)
-        inverse = lax.rsqrt(jnp.sum(sq[rows, :], axis=1, keepdims=True) * (1.0 / (NR * KB)) + EPSILON)
-        f = (acc[rows, :] * inverse + bias).astype(BF)
+        f = (acc[rows, :] + bias).astype(BF)
         slot = slot_of[i]
         q = qr[slot]
         s = lax.dot_general(q, f[:, :HS], NT_DIMS, preferred_element_type=F32) * SCALING
@@ -605,7 +623,6 @@
     V = pltpu.VMEM
     scratch = [
         V((8, ROWS, 2 * KB), BF),
-        V((KB, KVW), BF),
         V((NR, KB, KVW), BF),
         V((32, PAGE, KVW), BF),
         V((STEPS, RQ, 1024), BF),

time: 89.6 us -> 93.9 us (1.048)
  Pallas kernels: 87.7 us -> 92 us
    pallas_call x1, Pallas kernels: 87.7 us -> 92 us  [body(): pl.pallas_call(kernel, out_shape=jax.ShapeDtypeStruct((STEPS, 2 * RQ, NOU...]
where the time goes in v5:
time: 93.9 us; the launch traced here: 93.7 us
  Pallas kernels  92 us (98%)
  local copies, waits for them, and re-layouts  1.67 us (2%)
    pallas_call x1, Pallas kernels, body(): pl.pallas_call(kernel, out_shape=jax.ShapeDtypeStruct((STEPS, 2 * RQ, NOU...  92 us

profile of v5, /device:TPU:1, one launch (start us, length us, event | category | flops | bytes accessed | tf_op | source)
XLA Modules:
  0.0 93.7 jit_solution(11899559090550370047)
XLA Ops:
  0.0 92.0 %shard_map.118 = bf16[4,64,512]{2,1,0:T(8,128)(2,1)} custom-call(bf16[1408,8192]{1,0:T(8,128)(2,1)} %x_hbm.1, bf16[16,4,128]{2,1,0:T(4,128)(2,1)} %bitcast.6, bf16[512,256]{1,0:T(8,128)(2,1)} %w_hbm.1, bf16[2,128]{1,0:T(2,128)(2,1)} %bitcast.8, s32[1,11]{1,0:T(1,128)} %bitcast.9, s32[11]{0:T(128)} %req_ref.1, bf16[32,128,256]{2,1,0:T(8,128)(2,1)} %kv_hbm.1, ...), custom_call_target="tpu_custom_call" | custom-call | tf_op jit(solution)/shard_map/pallas_call | solution.py:679
  92.1 1.7 %copy.14 = bf16[4,64,512]{2,1,0:T(8,128)(2,1)} copy(bf16[4,64,512]{2,1,0:T(8,128)(2,1)} %shard_map.118) | data formatting | bytes 524288

commit v6 on v5

--- a/solution.py
+++ b/solution.py
@@ -226,17 +226,6 @@
     vtag[...] = tags
     rtag[me] = tags
 
-    dq_c.wait()
-    for s in range(STEPS):
-        for h in range(PER):
-            qf[pl.ds(s * PER + h, RQ, stride=RQ), :] = dq[s, :, h * HS : (h + 1) * HS].astype(F32)
-
-    def by_request(r, _):
-        qb[r] = qf[pl.ds(pl.multiple_of(r * RQ, RQ), RQ), :].astype(BF)
-        return 0
-
-    lax.fori_loop(0, RQ, by_request, 0, unroll=4)
-
     sq[...] = jnp.zeros_like(sq)
 
     def squares(i, _):
@@ -255,7 +244,6 @@
         lax.fori_loop(0, ROWS // SQ_TILE, tile, 0)
         return 0
 
-    lax.fori_loop(0, 4, squares, 0)
     w_c.wait()
 
     pl.semaphore_wait(barrier, NR - 1 + 3)
@@ -268,6 +256,17 @@
     lax.fori_loop(1, NR, send_tag, 0)
     w_all = Gather(lambda r: wv.at[r], lambda i: w_ss.at[i], lambda r: w_rs.at[r])
     w_all.first()
+
+    dq_c.wait()
+    for s in range(STEPS):
+        for h in range(PER):
+            qf[pl.ds(s * PER + h, RQ, stride=RQ), :] = dq[s, :, h * HS : (h + 1) * HS].astype(F32)
+
+    def by_request(r, _):
+        qb[r] = qf[pl.ds(pl.multiple_of(r * RQ, RQ), RQ), :].astype(BF)
+        return 0
+
+    lax.fori_loop(0, RQ, by_request, 0, unroll=4)
 
     def find_page(s, _):
         i = jnp.int32(0)
@@ -279,7 +278,7 @@
     lax.fori_loop(0, 2 * NR, find_page, 0)
 
     acc[...] = jnp.zeros_like(acc)
-    lax.fori_loop(4, 8, squares, 0)
+    lax.fori_loop(0, 8, squares, 0)
 
     def invert(t, _):
         rows = pl.ds(pl.multiple_of(t * PAGE, PAGE), PAGE)

time: 93.9 us -> 92.3 us (0.983)
  Pallas kernels: 92 us -> 90.4 us
    pallas_call x1, Pallas kernels: 92 us -> 90.4 us  [body(): pl.pallas_call(kernel, out_shape=jax.ShapeDtypeStruct((STEPS, 2 * RQ, NOU...]
where the time goes in v6:
time: 92.3 us; the launch traced here: 92.1 us
  Pallas kernels  90.4 us (98%)
  local copies, waits for them, and re-layouts  1.67 us (2%)
    pallas_call x1, Pallas kernels, body(): pl.pallas_call(kernel, out_shape=jax.ShapeDtypeStruct((STEPS, 2 * RQ, NOU...  90.4 us

profile of v6, /device:TPU:1, one launch (start us, length us, event | category | flops | bytes accessed | tf_op | source)
XLA Modules:
  0.0 92.1 jit_solution(16058522589685504018)
XLA Ops:
  0.0 90.4 %shard_map.118 = bf16[4,64,512]{2,1,0:T(8,128)(2,1)} custom-call(bf16[1408,8192]{1,0:T(8,128)(2,1)} %x_hbm.1, bf16[16,4,128]{2,1,0:T(4,128)(2,1)} %bitcast.6, bf16[512,256]{1,0:T(8,128)(2,1)} %w_hbm.1, bf16[2,128]{1,0:T(2,128)(2,1)} %bitcast.8, s32[1,11]{1,0:T(1,128)} %bitcast.9, s32[11]{0:T(128)} %req_ref.1, bf16[32,128,256]{2,1,0:T(8,128)(2,1)} %kv_hbm.1, ...), custom_call_target="tpu_custom_call" | custom-call | tf_op jit(solution)/shard_map/pallas_call | solution.py:678
  90.4 1.7 %copy.14 = bf16[4,64,512]{2,1,0:T(8,128)(2,1)} copy(bf16[4,64,512]{2,1,0:T(8,128)(2,1)} %shard_map.118) | data formatting | bytes 524288

commit v7 on v6

--- a/solution.py
+++ b/solution.py
@@ -26,7 +26,7 @@
 KVW = 256
 ROWS = NP * PAGE
 TILE = 704
-SQ_TILE = 176
+SQ_TILE = 352
 UNROLL = 4
 NOUT = 512
 SCALING = 1.0 / math.sqrt(HS)
@@ -565,17 +565,17 @@
         def _():
             product(i - 1)
 
+        @pl.when((i >= 3) & (i <= STEPS + 2))
+        def _():
+            add_x(i - 3)
+
+        @pl.when(i >= 4)
+        def _():
+            add_y(i - 4)
+
         @pl.when((i >= 2) & (i <= STEPS + 1))
         def _():
             relay_x(i - 2)
-
-        @pl.when((i >= 3) & (i <= STEPS + 2))
-        def _():
-            add_x(i - 3)
-
-        @pl.when(i >= 4)
-        def _():
-            add_y(i - 4)
 
         return 0
 

time: 92.3 us -> 93.9 us (1.017); the launches traced: 92.1 us -> 92.5 us
  no operation moved by 1% of the time
where the time goes in v7:
time: 93.9 us; the launch traced here: 92.5 us
  Pallas kernels  90.9 us (97%)
  local copies, waits for them, and re-layouts  1.67 us (2%)
    pallas_call x1, Pallas kernels, body(): pl.pallas_call(kernel, out_shape=jax.ShapeDtypeStruct((STEPS, 2 * RQ, NOU...  90.9 us

profile of v7, /device:TPU:1, one launch (start us, length us, event | category | flops | bytes accessed | tf_op | source)
XLA Modules:
  0.0 92.5 jit_solution(15955573333852780753)
XLA Ops:
  0.0 90.9 %shard_map.118 = bf16[4,64,512]{2,1,0:T(8,128)(2,1)} custom-call(bf16[1408,8192]{1,0:T(8,128)(2,1)} %x_hbm.1, bf16[16,4,128]{2,1,0:T(4,128)(2,1)} %bitcast.6, bf16[512,256]{1,0:T(8,128)(2,1)} %w_hbm.1, bf16[2,128]{1,0:T(2,128)(2,1)} %bitcast.8, s32[1,11]{1,0:T(1,128)} %bitcast.9, s32[11]{0:T(128)} %req_ref.1, bf16[32,128,256]{2,1,0:T(8,128)(2,1)} %kv_hbm.1, ...), custom_call_target="tpu_custom_call" | custom-call | tf_op jit(solution)/shard_map/pallas_call | solution.py:678
  90.9 1.7 %copy.14 = bf16[4,64,512]{2,1,0:T(8,128)(2,1)} copy(bf16[4,64,512]{2,1,0:T(8,128)(2,1)} %shard_map.118) | data formatting | bytes 524288
